TPU v7x, 32 devices: a whole 2x2x4 slice. The times are simulated.
32 devices in a mesh: row: 4 (over y, x), col: 8 (over z, core).
Axes of the slice: x: 2, y: 2, z: 4, core: 2. Of those that a mesh axis runs over, the one named last changes fastest.
Arguments:
- kernel_blocks: bfloat16 [64, 4, 256, 256], P('col', 'row'), may hold values from -6 to 6
- row_intersection: bfloat16 [512, 256, 256], P('col'), may hold values from -0.375 to 0.375
- col_intersection: bfloat16 [16, 256, 256], P('row'), may hold values from -0.375 to 0.375
- trial: bfloat16 [16, 64, 256], P('row', 'col'), may hold values from -0.09375 to 0.09375
- coarse_of_row: int32 [512], replicated, may hold values from 0 to 63, as said below
Outputs:
- fine_kernel: bfloat16 [512, 16, 256, 256], P('col', 'row')
- applied: bfloat16 [512, 64, 256], P(('col', 'row'))
Inputs may be any that keep to these rules, and one draw needn't show every extreme that they name: coarse_of_row never falls from one fine point to the next; coarse point 0 starts at fine point 0, and coarse point j >= 1 starts at fine point j * 8 - 512 // 128 + e_j with e_j between -3 and 3; every coarse point takes 1 to 15 consecutive fine points, and the last takes exactly 15.
All inputs are finite; a program needn't handle non-finite values.
Results may differ from a plain program's by a relative error of at most 0.0057.
Values may be sent and summed in bfloat16 or wider, within the bound.
No kernel may reach another device: no remote copies, remote signals or barrier semaphores. Data moves between devices by JAX's collectives and lax.ppermute only.
A program may use at most 128 MiB of HBM per device.

v0:
```python
import jax
import jax.numpy as jnp
from jax import lax
from jax.sharding import PartitionSpec as P


def from_behind(shard, axis, by):
    size = lax.axis_size(axis)
    pairs = [(i, i + by) for i in range(size) if 0 <= i + by < size]
    return lax.ppermute(shard, axis, pairs)


def per_device(kernel_blocks, row_intersection, col_intersection, trial, coarse_of_row):
    myself = lax.axis_index("col")
    rows_dev = row_intersection.shape[0]
    nc_dev = kernel_blocks.shape[0]
    owned = lax.dynamic_slice_in_dim(coarse_of_row, myself * rows_dev, rows_dev)
    local_blocks = kernel_blocks[:, 0]
    following = from_behind(local_blocks[0:1], "col", -1)
    available = jnp.concatenate([local_blocks, following], axis=0)
    right_avail = jnp.einsum(
        "nab,jbc->njac", available, col_intersection, preferred_element_type=jnp.float32
    ).astype(jnp.bfloat16)
    position = jnp.clip(owned - myself * nc_dev, 0, nc_dev)
    right = right_avail[position]
    fine_kernel = jnp.einsum(
        "kba,kjbc->kjac", row_intersection, right, preferred_element_type=jnp.float32
    ).astype(jnp.bfloat16)
    full_trial = lax.all_gather(trial, "col", axis=1, tiled=True)
    summed = lax.psum_scatter(
        jnp.einsum("kjab,jvb->kva", fine_kernel, full_trial, preferred_element_type=jnp.float32),
        "row",
        scatter_dimension=0,
        tiled=True,
    )
    applied = summed.astype(jnp.bfloat16)
    return (fine_kernel, applied)


def solution(mesh):
    in_specs = (
        P("col", "row", None, None),
        P("col", None, None),
        P("row", None, None),
        P("row", "col", None),
        P(),
    )
    out_specs = (P("col", "row", None, None), P(("col", "row"), None, None))
    return jax.shard_map(
        per_device, mesh=mesh, in_specs=in_specs, out_specs=out_specs, check_vma=False
    )
```

profile of v0, /device:TPU:1, one launch (start us, length us, event | category | flops | bytes accessed | tf_op | source)
XLA Modules:
  0.0 153.0 jit_solution(14486151414681395025)
XLA Ops:
  7.2 0.0 copy-start
  7.2 0.0 reduce-scatter.2.cloned.1.call-start
  7.2 1.0 slice_bitcast_fusion
  8.2 2.0 %collective-permute-start = (bf16[1,256,256]{2,1,0:T(8,128)(2,1)S(1)}, bf16[1,256,256]{2,1,0:T(8,128)(2,1)S(1)}, u32[]{:S(2)}, u32[]{:S(2)}) collective-permute-start(bf16[1,256,256]{2,1,0:T(8,128)(2,1)S(1)} %slice_bitcast_fusion), channel_id=1, source_target_pairs={{1,0},{2,1},{3,2},{4,3},{5,4},{6,5},{7,6},{9,8},{10,9},{11,10},{12... | collective-permute-start | bytes 393224 | tf_op jit(solution)/shard_map/ppermute | solution.py:10
  10.2 0.8 compare_select_fusion
  10.9 15.7 %all_gather.3 = bf16[4,64,256]{2,1,0:T(8,128)(2,1)S(1)} all-gather(bf16[4,8,256]{2,1,0:T(8,128)(2,1)} %param.8), channel_id=1, replica_groups=mesh['row'=4,'col'=8] {'col'}, dimensions={1}, use_global_device_ids=true | all-gather | bytes 147456 | tf_op jit(solution)/shard_map/all_gather | solution.py:29
  26.7 0.0 collective-permute-done
  26.7 0.0 copy-done
  26.7 4.7 %convert_bitcast_fusion.1 = bf16[9,4,256,256]{3,2,1,0:T(8,128)(2,1)} fusion(bf16[1,256,256]{2,1,0:T(8,128)(2,1)S(1)} %collective-permute-done, bf16[8,256,256]{2,1,0:T(8,128)(2,1)} %bitcast.30, bf16[4,256,256]{2,1,0:T(8,128)(2,1)S(1)} %copy-done), kind=kOutput, calls=%fused_computation.3 | convolution fusion | flops 1212678144 | bytes 6422528 | tf_op jit(solution)/shard_map/nab,jbc->njac/dot_general | solution.py:21
  31.4 15.0 %gather_fusion = bf16[64,4,256,256]{3,2,1,0:T(8,128)(2,1)} fusion(bf16[9,4,256,256]{3,2,1,0:T(8,128)(2,1)} %convert_bitcast_fusion.1, s32[1024]{0:T(1024)S(1)} %pad_clamp_fusion), kind=kCustom, calls=%fused_computation | custom fusion | bytes 67109120 | tf_op jit(solution)/shard_map/gather | solution.py:25
  46.4 28.6 %convert_bitcast_fusion = bf16[64,4,256,256]{2,3,1,0:T(8,128)(2,1)} fusion(bf16[64,4,256,256]{3,2,1,0:T(8,128)(2,1)} %gather_fusion, bf16[64,256,256]{2,1,0:T(8,128)(2,1)} %param.6), kind=kOutput, calls=%fused_computation.1 | convolution fusion | flops 8606711808 | bytes 75497472 | tf_op jit(solution)/shard_map/kba,kjbc->kjac/dot_general | solution.py:26
  75.1 15.6 %convolution_bitcast_fusion = f32[64,64,256]{2,1,0:T(8,128)} fusion(bf16[64,4,256,256]{2,3,1,0:T(8,128)(2,1)} %convert_bitcast_fusion, bf16[4,64,256]{2,1,0:T(8,128)(2,1)S(1)} %all_gather.3), kind=kOutput, calls=%fused_computation.4 | convolution fusion | flops 2147483648 | bytes 37879808 | tf_op jit(solution)/shard_map/kjab,jvb->kva/dot_general | solution.py:31
  90.7 0.0 reduce-scatter.2.cloned.1.call-update
  90.7 0.0 copy-start.1
  90.7 44.3 %copy.11 = bf16[64,4,256,256]{3,2,1,0:T(8,128)(2,1)} copy(bf16[64,4,256,256]{2,3,1,0:T(8,128)(2,1)} %convert_bitcast_fusion) | data formatting | bytes 67108864
  135.0 9.0 %reduce-scatter.2.cloned.1.call-done = f32[16,64,256]{2,1,0:T(8,128)} async-done(((f32[64,64,256]{2,1,0:T(8,128)}), f32[16,64,256]{2,1,0:T(8,128)}) %reduce-scatter.2.cloned.1.call-update) | async-done | bytes 1048592 | tf_op jit(solution)/shard_map/reduce_scatter | solution.py:30
  144.1 2.1 %convert_element_type.19 = bf16[16,64,256]{2,1,0:T(8,128)(2,1)} convert(f32[16,64,256]{2,1,0:T(8,128)} %reduce-scatter.2.cloned.1.call-done) | non-fusion elementwise | flops 262144 | bytes 1572864 | tf_op jit(solution)/shard_map/convert_element_type | solution.py:36
  146.1 0.0 copy-done.1
  (1 shorter events, 0.0 us)
Async XLA Ops:
  7.2 19.5 %copy-start = (bf16[4,256,256]{2,1,0:T(8,128)(2,1)S(1)}, bf16[4,256,256]{2,1,0:T(8,128)(2,1)}, u32[]{:S(2)}) copy-start(bf16[4,256,256]{2,1,0:T(8,128)(2,1)} %param.7) | copy-start | bytes 1572868
  7.2 136.9 %reduce-scatter.2.cloned.1.call-start = ((), (), s32[]{:S(2)}) async-start(), calls=%async_computation.1 | async-start | bytes 5242880 | tf_op jit(solution)/shard_map/reduce_scatter | solution.py:30
  8.2 18.5 %collective-permute-start = (bf16[1,256,256]{2,1,0:T(8,128)(2,1)S(1)}, bf16[1,256,256]{2,1,0:T(8,128)(2,1)S(1)}, u32[]{:S(2)}, u32[]{:S(2)}) collective-permute-start(bf16[1,256,256]{2,1,0:T(8,128)(2,1)S(1)} %slice_bitcast_fusion), channel_id=1, source_target_pairs={{1,0},{2,1},{3,2},{4,3},{5,4},{6,5},{7,6},{9,8},{10,9},{11,10},{12... | collective-permute-start | bytes 393224 | tf_op jit(solution)/shard_map/ppermute | solution.py:10
  90.7 55.4 %copy-start.1 = (bf16[4,256,256]{2,1,0:T(8,128)(2,1)S(1)}, bf16[4,256,256]{2,1,0:T(8,128)(2,1)}, u32[]{:S(2)}) copy-start(bf16[4,256,256]{2,1,0:T(8,128)(2,1)} %param.7) | copy-start | bytes 1572868
Sparse Core Ops, SparseCore 0:
  90.8 53.1 reduce-scatter.1
where the time goes:
time: 155 us; the launch traced here: 153 us
  local copies, waits for them, and re-layouts  60.3 us (39%)
  matrix products  49 us (32%)
  blocking collectives  15.7 us (10%)
  between operations  14.1 us (9%)
  waiting for transfers between devices  9.07 us (6%)
  other arithmetic  2.85 us (2%)
  starting transfers between devices  2 us (1%)
    unnamed x5, local copies, waits for them, and re-layouts  44.3 us
    dot_general x1, matrix products, per_device(): jnp.einsum('kba,kjbc->kjac', row_intersection, right, preferred_element_t...  28.6 us
    all_gather x1, blocking collectives, per_device(): full_trial = lax.all_gather(trial, 'col', axis=1, tiled=True)  15.7 us
    dot_general x1, matrix products, per_device(): jnp.einsum('kjab,jvb->kva', fine_kernel, full_trial, preferred_element_ty...  15.6 us
    gather x1, local copies, waits for them, and re-layouts, per_device(): right = right_avail[position]  15 us
    reduce_scatter x1, waiting for transfers between devices, per_device(): lax.psum_scatter(jnp.einsum('kjab,jvb->kva', fine_kernel, full_trial, pre...  9.05 us
    dot_general x1, matrix products, per_device(): jnp.einsum('nab,jbc->njac', available, col_intersection, preferred_elemen...  4.74 us
  transfers between devices with their start and end apart: 2, of which 1 were waited for; matrix products, arithmetic and copies ran while one was open for 29% of the time, Pallas kernels for 0%

commit v1 on v0

v1 whole, which is shorter than its diff:
```python
import functools

import jax
import jax.numpy as jnp
from jax import lax
from jax.experimental import pallas as pl
from jax.experimental.pallas import tpu as pltpu
from jax.sharding import PartitionSpec as P

BF = jnp.bfloat16
F32 = jnp.float32
MIB = 1024 * 1024
NT = (((1,), (1,)), ((), ()))
NN = (((1,), (0,)), ((), ()))


def dot(x, y, dims=NN):
    return lax.dot_general(x, y, dims, preferred_element_type=F32)


def two_terms(x):
    high = x.astype(BF)
    low = (x - high.astype(F32)).astype(BF)
    return jnp.concatenate([high, low], axis=0)


def folded_dot(x, y, dims=NN):
    z = dot(x, y, dims)
    half = z.shape[0] // 2
    return z[:half] + z[half:]


def rows_kernel(spacing, per, coarse, c_ref, k_ref, f_ref, u_ref, _, out, r_v, o_v, osem):
    nc = k_ref.shape[0]
    m = c_ref.shape[0]
    base_j = lax.axis_index("col") * nc
    base_k = lax.axis_index("col") * nc * spacing

    def right(j, block):
        for q in range(m):
            r_v[j, q] = dot(block, c_ref[q]).astype(BF)

    def write(k):
        return pltpu.make_async_copy(o_v.at[k], out.at[k], osem.at[k])

    def rows(i):
        for t in range(per * spacing):
            k = i * spacing + t
            at = jnp.clip(coarse[base_k + k] - base_j, 0, nc)
            ut = u_ref[k].T
            for q in range(m):
                o_v[k, q] = dot(ut, r_v[at, q]).astype(BF)
            write(k).start()

    right(nc, f_ref[0, 0])
    for j in range(min(per + 1, nc)):
        right(j, k_ref[j, 0])

    def step(n, carry):
        rows(n * per)
        for j in range(per):
            ahead = jnp.minimum(n * per + per + 1 + j, nc - 1)
            right(ahead, k_ref[ahead, 0])
        return carry

    lax.fori_loop(0, nc // per - 1, step, 0)
    rows(nc - per)
    for k in range(nc * spacing):
        write(k).wait()


def fine_rows(spacing, coarse, c, kb, following, u, after):
    rows, p, _ = u.shape
    nc, m = kb.shape[0], c.shape[0]
    per = 2 if nc % 2 == 0 else 1
    vmem = pl.BlockSpec(memory_space=pltpu.VMEM)
    return pl.pallas_call(
        functools.partial(rows_kernel, spacing, per),
        out_shape=jax.ShapeDtypeStruct((rows, m, p, p), BF),
        in_specs=[pl.BlockSpec(memory_space=pltpu.SMEM)] + [vmem] * 4 + [pl.BlockSpec(memory_space=pl.ANY)],
        out_specs=pl.BlockSpec(memory_space=pl.ANY),
        scratch_shapes=[
            pltpu.VMEM((nc + 1, m, p, p), BF),
            pltpu.VMEM((rows, m, p, p), BF),
            pltpu.SemaphoreType.DMA((rows,)),
        ],
        compiler_params=pltpu.CompilerParams(vmem_limit_bytes=50 * MIB),
        cost_estimate=pl.CostEstimate(
            flops=2 * rows * m * p**3, bytes_accessed=2 * rows * (m + 1) * p * p, transcendentals=0
        ),
        name="fine_rows",
    )(coarse, c, kb, following, u, after)


def shares_kernel(lows, n_row, n_col, c_ref, k_ref, f_ref, t_ref, own_ref, *refs):
    sends, w_v = refs[: n_row - 1], refs[-1]
    m, nv = t_ref.shape[:2]
    nc = k_ref.shape[0]
    s = two_terms(sum(dot(t_ref[q], c_ref[q], NT) for q in range(m)))
    each, half = nv // n_col, n_col // 2
    at = lax.broadcasted_iota(jnp.int32, (nv, nv), 1)
    block = lax.div(at, each)
    source = lax.bitwise_xor(lax.axis_index("col"), 2 * lax.rem(block, half) + lax.div(block, half))
    place = source * each + lax.rem(at, each)
    order = (place == lax.broadcasted_iota(jnp.int32, (nv, nv), 0)).astype(F32).astype(BF)
    s = jnp.concatenate([dot(order, s[:nv]), dot(order, s[nv:])], axis=0).astype(BF)
    for j in range(nc + 1):
        w_v[j] = folded_dot(s, k_ref[j, 0] if j < nc else f_ref[0, 0], NT)
    me = lax.axis_index("row")
    (own, spacing), width = lows
    own_ref[...] = w_v[pl.ds(me * own // spacing, width)]
    for n in range(1, n_row):
        other = lax.bitwise_xor(me, n)
        sends[n - 1][...] = w_v[pl.ds(other * own // spacing, width)].astype(BF)


def shares(lows, n_row, n_col, c, kb, following, t):
    nv, p = t.shape[1:]
    width = lows[1]
    vmem = pl.BlockSpec(memory_space=pltpu.VMEM)
    return pl.pallas_call(
        functools.partial(shares_kernel, lows, n_row, n_col),
        out_shape=[jax.ShapeDtypeStruct((width, nv, p), F32)]
        + [jax.ShapeDtypeStruct((width, nv, p), BF)] * (n_row - 1),
        in_specs=[vmem] * 4,
        out_specs=[vmem] * n_row,
        scratch_shapes=[pltpu.VMEM((kb.shape[0] + 1, nv, p), F32)],
        compiler_params=pltpu.CompilerParams(vmem_limit_bytes=16 * MIB),
        name="row_shares",
    )(c, kb, following, t)


def applied_kernel(lows, n_row, nc, spacing, coarse, u_ref, own_ref, *refs):
    got = refs[: n_row - 1]
    out, w_v = refs[-2:]
    (own, _), width = lows
    me = lax.axis_index("row")
    base_j = lax.axis_index("col") * nc + me * own // spacing
    base_k = lax.axis_index("col") * nc * spacing + me * own
    w = own_ref[...]
    for ref in got:
        w = w + ref[...].astype(F32)
    for i in range(width):
        w_v[i] = two_terms(w[i])
    for t in range(own):
        at = jnp.clip(coarse[base_k + t] - base_j, 0, width - 1)
        out[t] = folded_dot(w_v[at], u_ref[me * own + t]).astype(BF)


def applied_rows(lows, n_row, nc, spacing, coarse, u, own_share, got, after):
    width, nv, p = own_share.shape
    vmem = pl.BlockSpec(memory_space=pltpu.VMEM)
    return pl.pallas_call(
        functools.partial(applied_kernel, lows, n_row, nc, spacing),
        out_shape=jax.ShapeDtypeStruct((lows[0][0], nv, p), BF),
        in_specs=[pl.BlockSpec(memory_space=pltpu.SMEM)] + [vmem] * (n_row + 1),
        out_specs=vmem,
        scratch_shapes=[pltpu.VMEM((width, 2 * nv, p), BF)],
        compiler_params=pltpu.CompilerParams(vmem_limit_bytes=24 * MIB),
        name="applied_rows",
    )(coarse, u, own_share, *got)


def gather_trial(trial):
    n = lax.axis_size("col")

    def swap(x, by):
        return lax.ppermute(x, "col", [(i, i ^ by) for i in range(n)])

    half = jnp.concatenate([trial] + [swap(trial, by) for by in range(2, n, 2)], axis=1)
    return jnp.concatenate([half, swap(half, 1)], axis=1)


def per_device(kb, u, c, trial, coarse):
    n_row, n_col = lax.axis_size("row"), lax.axis_size("col")
    nc, rows = kb.shape[0], u.shape[0]
    spacing = rows // nc
    own = rows // n_row
    width = max((r * own + own - 1) // spacing + 2 - r * own // spacing for r in range(n_row))
    lows = ((own, spacing), width)
    full = gather_trial(trial)
    following = lax.ppermute(kb[0:1], "col", [(i + 1, i) for i in range(n_col - 1)])
    own_share, *sends = shares(lows, n_row, n_col, c, kb, following, full)
    got = [lax.ppermute(x, "row", [(i, i ^ (n + 1)) for i in range(n_row)]) for n, x in enumerate(sends)]
    fine = fine_rows(spacing, coarse, c, kb, following, u, own_share)
    applied = applied_rows(lows, n_row, nc, spacing, coarse, u, own_share, got, fine)
    return fine, applied


def solution(mesh):
    in_specs = (
        P("col", "row", None, None),
        P("col", None, None),
        P("row", None, None),
        P("row", "col", None),
        P(),
    )
    out_specs = (P("col", "row", None, None), P(("col", "row"), None, None))
    return jax.shard_map(
        per_device, mesh=mesh, in_specs=in_specs, out_specs=out_specs, check_vma=False
    )
```

time: 155 us -> 41.2 us (0.27)
  the two profiles are of different devices: /device:TPU:1 before, /device:TPU:0 now
where the time goes in v1:
time: 41.2 us; the launch traced here: 40.7 us
  Pallas kernels  19.2 us (47%)
  starting transfers between devices  10.6 us (26%)
  local copies, waits for them, and re-layouts  6.87 us (17%)
  waiting for transfers between devices  2.5 us (6%)
  between operations  0.75 us (2%)
  other arithmetic  0.72 us (2%)
    pallas_call x1, Pallas kernels, fine_rows(): pl.pallas_call(functools.partial(rows_kernel, spacing, per), out_shape=ja...  16.2 us
    unnamed x18, local copies, waits for them, and re-layouts  5.95 us
    ppermute x4, starting transfers between devices, swap(): return lax.ppermute(x, 'col', [(i, i ^ by) for i in range(n)])  5.76 us
    ppermute x3, starting transfers between devices, per_device(): lax.ppermute(x, 'row', [(i, i ^ n + 1) for i in range(n_row)])  3.55 us
    ppermute x4, waiting for transfers between devices, swap(): return lax.ppermute(x, 'col', [(i, i ^ by) for i in range(n)])  2.49 us
    pallas_call x1, Pallas kernels, applied_rows(): pl.pallas_call(functools.partial(applied_kernel, lows, n_row, nc, spacing...  1.89 us
    ppermute x1, starting transfers between devices, per_device(): lax.ppermute(kb[0:1], 'col', [(i + 1, i) for i in range(n_col - 1)])  1.29 us
    pallas_call x1, Pallas kernels, shares(): pl.pallas_call(functools.partial(shares_kernel, lows, n_row, n_col), out_...  1.13 us
  transfers between devices with their start and end apart: 8, of which 2 were waited for; matrix products, arithmetic and copies ran while one was open for 6% of the time, Pallas kernels for 40%

profile of v1, /device:TPU:0, one launch (start us, length us, event | category | flops | bytes accessed | tf_op | source)
XLA Modules:
  0.0 40.7 jit_solution(11094757987192125517)
XLA Ops:
  0.6 0.0 slice-start
  0.6 5.1 %collective-permute-start.3 = (bf16[4,8,256]{2,1,0:T(8,128)(2,1)}, bf16[4,8,256]{2,1,0:T(8,128)(2,1)S(1)}, u32[]{:S(2)}, u32[]{:S(2)}) collective-permute-start(bf16[4,8,256]{2,1,0:T(8,128)(2,1)} %param.8), channel_id=1, source_target_pairs={{0,6},{1,7},{2,4},{3,5},{4,2},{5,3},{6,0},{7,1},{8,14},{9,15},{10,... | collective-permute-start | bytes 49160 | tf_op jit(solution)/shard_map/ppermute | solution.py:168
  5.8 0.0 collective-permute-start.2
  5.8 0.6 %collective-permute-start.1 = (bf16[4,8,256]{2,1,0:T(8,128)(2,1)}, bf16[4,8,256]{2,1,0:T(8,128)(2,1)S(1)}, u32[]{:S(2)}, u32[]{:S(2)}) collective-permute-start(bf16[4,8,256]{2,1,0:T(8,128)(2,1)} %param.8), channel_id=1, source_target_pairs={{0,2},{1,3},{2,0},{3,1},{4,6},{5,7},{6,4},{7,5},{8,10},{9,11},{10,... | collective-permute-start | bytes 49160 | tf_op jit(solution)/shard_map/ppermute | solution.py:168
  6.4 0.9 %slice.3 = bf16[1,1,256,256]{3,2,1,0:T(8,128)(2,1)S(1)} slice(bf16[8,1,256,256]{3,2,1,0:T(8,128)(2,1)} %k_ref.3), slice={[0:1], [0:1], [0:256], [0:256]} | slice | bytes 262144 | tf_op jit(solution)/shard_map/slice | solution.py:182
  7.3 1.3 %collective-permute-start = (bf16[1,1,256,256]{3,2,1,0:T(8,128)(2,1)S(1)}, bf16[1,1,256,256]{3,2,1,0:T(8,128)(2,1)S(1)}, u32[]{:S(2)}, u32[]{:S(2)}) collective-permute-start(bf16[1,1,256,256]{3,2,1,0:T(8,128)(2,1)S(1)} %slice.3), channel_id=1, source_target_pairs={{1,0},{2,1},{3,2},{4,3},{5,4},{6,5},{7,6},{9,8},{10,9},{11,10},{12... | collective-permute-start | bytes 393224 | tf_op jit(solution)/shard_map/ppermute | solution.py:182
  8.6 0.7 %constant_dynamic-update-slice_fusion.4 = bf16[4,64,256]{2,1,0:T(8,128)(2,1)S(1)} fusion(bf16[4,8,256]{2,1,0:T(8,128)(2,1)} %param.8), kind=kLoop, calls=%fused_computation.5 | loop fusion | bytes 32768
  9.3 0.0 collective-permute-done.3
  9.3 1.3 %collective-permute-done.2 = bf16[4,8,256]{2,1,0:T(8,128)(2,1)S(1)} collective-permute-done((bf16[4,8,256]{2,1,0:T(8,128)(2,1)}, bf16[4,8,256]{2,1,0:T(8,128)(2,1)S(1)}, u32[]{:S(2)}, u32[]{:S(2)}) %collective-permute-start.2) | collective-permute-done | bytes 16416 | tf_op jit(solution)/shard_map/ppermute | solution.py:168
  10.6 0.0 collective-permute-done.1
  10.6 0.7 %pad_maximum_fusion = bf16[4,32,256]{2,1,0:T(8,128)(2,1)S(1)} fusion(bf16[4,8,256]{2,1,0:T(8,128)(2,1)S(1)} %collective-permute-done.3, bf16[4,8,256]{2,1,0:T(8,128)(2,1)S(1)} %collective-permute-done.2, bf16[4,8,256]{2,1,0:T(8,128)(2,1)S(1)} %collective-permute-done.1, bf16[4,8,256]{2,1,0:T(8,128)(2,1)} %param.8), kind=kLoop, calls=%fused_computation | loop fusion | flops 262144 | bytes 131072 | tf_op jit(solution)/shard_map/concatenate | solution.py:170
  11.3 0.0 collective-permute-start.4
  11.4 1.2 %collective-permute-done.4 = bf16[4,32,256]{2,1,0:T(8,128)(2,1)S(1)} collective-permute-done((bf16[4,32,256]{2,1,0:T(8,128)(2,1)S(1)}, bf16[4,32,256]{2,1,0:T(8,128)(2,1)S(1)}, u32[]{:S(2)}, u32[]{:S(2)}) %collective-permute-start.4) | collective-permute-done | bytes 65568 | tf_op jit(solution)/shard_map/ppermute | solution.py:168
  12.6 0.0 collective-permute-done.f_ref
  12.6 0.0 copy-start
  12.6 1.2 %copy-done = bf16[8,1,256,256]{3,2,1,0:T(8,128)(2,1)S(1)} copy-done((bf16[8,1,256,256]{3,2,1,0:T(8,128)(2,1)S(1)}, bf16[8,1,256,256]{3,2,1,0:T(8,128)(2,1)}, u32[]{:S(2)}) %copy-start) | copy-done | bytes 1048600
  13.8 0.0 copy-start.2
  13.8 1.0 %copy-done.2 = bf16[4,256,256]{2,1,0:T(8,128)(2,1)S(1)} copy-done((bf16[4,256,256]{2,1,0:T(8,128)(2,1)S(1)}, bf16[4,256,256]{2,1,0:T(8,128)(2,1)}, u32[]{:S(2)}) %copy-start.2) | copy-done | bytes 524312
  14.9 1.1 %row_shares.1 = (f32[3,64,256]{2,1,0:T(8,128)S(1)}, bf16[3,64,256]{2,1,0:T(8,128)(2,1)S(1)}, bf16[3,64,256]{2,1,0:T(8,128)(2,1)S(1)}, bf16[3,64,256]{2,1,0:T(8,128)(2,1)S(1)}) custom-call(bf16[4,256,256]{2,1,0:T(8,128)(2,1)S(1)} %copy-done.2, bf16[8,1,256,256]{3,2,1,0:T(8,128)(2,1)S(1)} %copy-done, bf16[1,1,256,256]{3,2,1,0:T(8,128)(2,1)S(1)} %collective-permute-done.f_ref, ...), custom_call_target="tpu_custom_call" | custom-call | tf_op jit(solution)/shard_map/row_shares/pallas_call | solution.py:121
  16.0 1.6 %collective-permute-start.5 = (bf16[3,64,256]{2,1,0:T(8,128)(2,1)S(1)}, bf16[3,64,256]{2,1,0:T(8,128)(2,1)S(1)}, u32[]{:S(2)}, u32[]{:S(2)}) collective-permute-start(bf16[3,64,256]{2,1,0:T(8,128)(2,1)S(1)} %get-tuple-element.7), channel_id=1, source_target_pairs={{0,8},{8,0},{16,24},{24,16},{1,9},{9,1},{17,25},{25,17},{2,10},{10... | collective-permute-start | bytes 294920 | tf_op jit(solution)/shard_map/ppermute | solution.py:184
  17.6 1.5 %collective-permute-start.6 = (bf16[3,64,256]{2,1,0:T(8,128)(2,1)S(1)}, bf16[3,64,256]{2,1,0:T(8,128)(2,1)S(1)}, u32[]{:S(2)}, u32[]{:S(2)}) collective-permute-start(bf16[3,64,256]{2,1,0:T(8,128)(2,1)S(1)} %get-tuple-element.8), channel_id=1, source_target_pairs={{0,16},{8,24},{16,0},{24,8},{1,17},{9,25},{17,1},{25,9},{2,18},{10... | collective-permute-start | bytes 294920 | tf_op jit(solution)/shard_map/ppermute | solution.py:184
  19.1 0.5 %collective-permute-start.7 = (bf16[3,64,256]{2,1,0:T(8,128)(2,1)S(1)}, bf16[3,64,256]{2,1,0:T(8,128)(2,1)S(1)}, u32[]{:S(2)}, u32[]{:S(2)}) collective-permute-start(bf16[3,64,256]{2,1,0:T(8,128)(2,1)S(1)} %get-tuple-element.9), channel_id=1, source_target_pairs={{0,24},{8,16},{16,8},{24,0},{1,25},{9,17},{17,9},{25,1},{2,26},{10... | collective-permute-start | bytes 294920 | tf_op jit(solution)/shard_map/ppermute | solution.py:184
  19.6 0.0 copy-start.1
  19.6 1.2 %copy-done.1 = bf16[8,1,256,256]{3,2,1,0:T(8,128)(2,1)S(1)} copy-done((bf16[8,1,256,256]{3,2,1,0:T(8,128)(2,1)S(1)}, bf16[8,1,256,256]{3,2,1,0:T(8,128)(2,1)}, u32[]{:S(2)}) %copy-start.1) | copy-done | bytes 1048600
  20.8 0.0 copy-start.3
  20.8 1.0 %copy-done.3 = bf16[4,256,256]{2,1,0:T(8,128)(2,1)S(1)} copy-done((bf16[4,256,256]{2,1,0:T(8,128)(2,1)S(1)}, bf16[4,256,256]{2,1,0:T(8,128)(2,1)}, u32[]{:S(2)}) %copy-start.3) | copy-done | bytes 524312
  21.8 0.0 copy-start.4
  21.8 0.7 %copy-done.4 = s32[512]{0:T(512)S(1)} copy-done((s32[512]{0:T(512)S(1)}, s32[512]{0:T(512)}, u32[]{:S(2)}) %copy-start.4) | copy-done | bytes 2072
  22.5 0.0 slice-start.1
  22.5 16.2 %fine_rows.1 = bf16[64,4,256,256]{3,2,1,0:T(8,128)(2,1)} custom-call(s32[512]{0:T(512)S(1)} %copy-done.4, bf16[4,256,256]{2,1,0:T(8,128)(2,1)S(1)} %copy-done.3, bf16[8,1,256,256]{3,2,1,0:T(8,128)(2,1)S(1)} %copy-done.1, bf16[1,1,256,256]{3,2,1,0:T(8,128)(2,1)S(1)} %collective-permute-done.f_ref, bf16[64,256,256]{2,1,0:T(8,128)(2,1)} %u_ref.3, ...), custom_call_target="tpu_custom_call" | custom-call | flops 8589934592 | bytes 41943040 | tf_op jit(solution)/shard_map/fine_rows/pallas_call | solution.py:77
  38.7 0.0 collective-permute-done.5.refs_0_
  38.8 0.0 collective-permute-done.6.refs_1_
  38.8 0.0 collective-permute-done.7.refs_2_
  38.8 0.0 slice-done
  38.8 0.0 slice-done.1
  38.8 1.9 %applied_rows.1 = bf16[16,64,256]{2,1,0:T(8,128)(2,1)} custom-call(s32[512]{0:T(512)S(1)} %copy-done.4, bf16[64,256,256]{2,1,0:T(8,128)(2,1)S(1)} %bitcast.1, f32[3,64,256]{2,1,0:T(8,128)S(1)} %get-tuple-element.6._.own_ref, bf16[3,64,256]{2,1,0:T(8,128)(2,1)S(1)} %collective-permute-done.5.refs_0_, bf16[3,64,256]{2,1,0:T(8,128)(2,1)S(1)} %collective-permute-done.6.refs_1_, ...), custom_call_target="tpu_custom_call" | custom-call | tf_op jit(solution)/shard_map/applied_rows/pallas_call | solution.py:153
  (5 shorter events, 0.0 us)
Async XLA Ops:
  0.6 38.2 %slice-start = ((s8[8388608]{0:T(1024)(128)(4,1)}), s8[4194304]{0:T(1024)(128)(4,1)S(1)}, s32[]{:S(2)}) async-start(s8[8388608]{0:T(1024)(128)(4,1)} %bitcast), calls=%async_computation | async-start | bytes 8388608
  0.6 8.7 %collective-permute-start.3 = (bf16[4,8,256]{2,1,0:T(8,128)(2,1)}, bf16[4,8,256]{2,1,0:T(8,128)(2,1)S(1)}, u32[]{:S(2)}, u32[]{:S(2)}) collective-permute-start(bf16[4,8,256]{2,1,0:T(8,128)(2,1)} %param.8), channel_id=1, source_target_pairs={{0,6},{1,7},{2,4},{3,5},{4,2},{5,3},{6,0},{7,1},{8,14},{9,15},{10,... | collective-permute-start | bytes 49160 | tf_op jit(solution)/shard_map/ppermute | solution.py:168
  5.8 4.8 %collective-permute-start.2 = (bf16[4,8,256]{2,1,0:T(8,128)(2,1)}, bf16[4,8,256]{2,1,0:T(8,128)(2,1)S(1)}, u32[]{:S(2)}, u32[]{:S(2)}) collective-permute-start(bf16[4,8,256]{2,1,0:T(8,128)(2,1)} %param.8), channel_id=1, source_target_pairs={{0,4},{1,5},{2,6},{3,7},{4,0},{5,1},{6,2},{7,3},{8,12},{9,13},{10,... | collective-permute-start | bytes 49160 | tf_op jit(solution)/shard_map/ppermute | solution.py:168
  5.8 4.8 %collective-permute-start.1 = (bf16[4,8,256]{2,1,0:T(8,128)(2,1)}, bf16[4,8,256]{2,1,0:T(8,128)(2,1)S(1)}, u32[]{:S(2)}, u32[]{:S(2)}) collective-permute-start(bf16[4,8,256]{2,1,0:T(8,128)(2,1)} %param.8), channel_id=1, source_target_pairs={{0,2},{1,3},{2,0},{3,1},{4,6},{5,7},{6,4},{7,5},{8,10},{9,11},{10,... | collective-permute-start | bytes 49160 | tf_op jit(solution)/shard_map/ppermute | solution.py:168
  7.3 5.3 %collective-permute-start = (bf16[1,1,256,256]{3,2,1,0:T(8,128)(2,1)S(1)}, bf16[1,1,256,256]{3,2,1,0:T(8,128)(2,1)S(1)}, u32[]{:S(2)}, u32[]{:S(2)}) collective-permute-start(bf16[1,1,256,256]{3,2,1,0:T(8,128)(2,1)S(1)} %slice.3), channel_id=1, source_target_pairs={{1,0},{2,1},{3,2},{4,3},{5,4},{6,5},{7,6},{9,8},{10,9},{11,10},{12... | collective-permute-start | bytes 393224 | tf_op jit(solution)/shard_map/ppermute | solution.py:182
  11.3 1.3 %collective-permute-start.4 = (bf16[4,32,256]{2,1,0:T(8,128)(2,1)S(1)}, bf16[4,32,256]{2,1,0:T(8,128)(2,1)S(1)}, u32[]{:S(2)}, u32[]{:S(2)}) collective-permute-start(bf16[4,32,256]{2,1,0:T(8,128)(2,1)S(1)} %pad_maximum_fusion), channel_id=1, source_target_pairs={{0,1},{1,0},{2,3},{3,2},{4,5},{5,4},{6,7},{7,6},{8,9},{9,8},{10,11... | collective-permute-start | bytes 196616 | tf_op jit(solution)/shard_map/ppermute | solution.py:168
  12.6 1.2 %copy-start = (bf16[8,1,256,256]{3,2,1,0:T(8,128)(2,1)S(1)}, bf16[8,1,256,256]{3,2,1,0:T(8,128)(2,1)}, u32[]{:S(2)}) copy-start(bf16[8,1,256,256]{3,2,1,0:T(8,128)(2,1)} %k_ref.3) | copy-start | bytes 3145732
  13.8 1.0 %copy-start.2 = (bf16[4,256,256]{2,1,0:T(8,128)(2,1)S(1)}, bf16[4,256,256]{2,1,0:T(8,128)(2,1)}, u32[]{:S(2)}) copy-start(bf16[4,256,256]{2,1,0:T(8,128)(2,1)} %c_ref.3) | copy-start | bytes 1572868
  16.0 22.7 %collective-permute-start.5 = (bf16[3,64,256]{2,1,0:T(8,128)(2,1)S(1)}, bf16[3,64,256]{2,1,0:T(8,128)(2,1)S(1)}, u32[]{:S(2)}, u32[]{:S(2)}) collective-permute-start(bf16[3,64,256]{2,1,0:T(8,128)(2,1)S(1)} %get-tuple-element.7), channel_id=1, source_target_pairs={{0,8},{8,0},{16,24},{24,16},{1,9},{9,1},{17,25},{25,17},{2,10},{10... | collective-permute-start | bytes 294920 | tf_op jit(solution)/shard_map/ppermute | solution.py:184
  17.6 21.2 %collective-permute-start.6 = (bf16[3,64,256]{2,1,0:T(8,128)(2,1)S(1)}, bf16[3,64,256]{2,1,0:T(8,128)(2,1)S(1)}, u32[]{:S(2)}, u32[]{:S(2)}) collective-permute-start(bf16[3,64,256]{2,1,0:T(8,128)(2,1)S(1)} %get-tuple-element.8), channel_id=1, source_target_pairs={{0,16},{8,24},{16,0},{24,8},{1,17},{9,25},{17,1},{25,9},{2,18},{10... | collective-permute-start | bytes 294920 | tf_op jit(solution)/shard_map/ppermute | solution.py:184
  19.1 19.7 %collective-permute-start.7 = (bf16[3,64,256]{2,1,0:T(8,128)(2,1)S(1)}, bf16[3,64,256]{2,1,0:T(8,128)(2,1)S(1)}, u32[]{:S(2)}, u32[]{:S(2)}) collective-permute-start(bf16[3,64,256]{2,1,0:T(8,128)(2,1)S(1)} %get-tuple-element.9), channel_id=1, source_target_pairs={{0,24},{8,16},{16,8},{24,0},{1,25},{9,17},{17,9},{25,1},{2,26},{10... | collective-permute-start | bytes 294920 | tf_op jit(solution)/shard_map/ppermute | solution.py:184
  19.6 1.2 %copy-start.1 = (bf16[8,1,256,256]{3,2,1,0:T(8,128)(2,1)S(1)}, bf16[8,1,256,256]{3,2,1,0:T(8,128)(2,1)}, u32[]{:S(2)}) copy-start(bf16[8,1,256,256]{3,2,1,0:T(8,128)(2,1)} %k_ref.3) | copy-start | bytes 3145732
  20.8 1.0 %copy-start.3 = (bf16[4,256,256]{2,1,0:T(8,128)(2,1)S(1)}, bf16[4,256,256]{2,1,0:T(8,128)(2,1)}, u32[]{:S(2)}) copy-start(bf16[4,256,256]{2,1,0:T(8,128)(2,1)} %c_ref.3) | copy-start | bytes 1572868
  21.8 0.7 %copy-start.4 = (s32[512]{0:T(512)S(1)}, s32[512]{0:T(512)}, u32[]{:S(2)}) copy-start(s32[512]{0:T(512)} %coarse.3) | copy-start | bytes 6148
  22.5 16.3 %slice-start.1 = ((s8[8388608]{0:T(1024)(128)(4,1)}), s8[4194304]{0:T(1024)(128)(4,1)S(1)}, s32[]{:S(2)}) async-start(s8[8388608]{0:T(1024)(128)(4,1)} %bitcast), calls=%async_computation.1 | async-start | bytes 8388608

commit v2 on v1

v2 whole, which is shorter than its diff:
```python
import functools

import jax
import jax.numpy as jnp
from jax import lax
from jax.experimental import pallas as pl
from jax.experimental.pallas import tpu as pltpu
from jax.sharding import PartitionSpec as P

BF = jnp.bfloat16
F32 = jnp.float32
MIB = 1024 * 1024
NT = (((1,), (1,)), ((), ()))
NN = (((1,), (0,)), ((), ()))


def dot(x, y, dims=NN):
    return lax.dot_general(x, y, dims, preferred_element_type=F32)


def two_terms(x):
    high = x.astype(BF)
    low = (x - high.astype(F32)).astype(BF)
    return jnp.concatenate([high, low], axis=0)


def folded_dot(x, y, dims=NN):
    z = dot(x, y, dims)
    half = z.shape[0] // 2
    return z[:half] + z[half:]


def ready_kernel(spacing, c_hbm, k_hbm, u_hbm, t_hbm, coarse_hbm, c_v, k_v, u_v, t_v, coarse_v, first_v, r_v, csem, tsem, osem, ksem, usem):
    nc = k_hbm.shape[0]

    def load_k(j):
        return pltpu.make_async_copy(k_hbm.at[j, 0], k_v.at[j], ksem.at[j])

    def load_u(j):
        here = pl.ds(j * spacing, spacing)
        return pltpu.make_async_copy(u_hbm.at[here], u_v.at[here], usem.at[j])

    small = [
        pltpu.make_async_copy(c_hbm, c_v, csem),
        pltpu.make_async_copy(t_hbm, t_v, tsem),
        pltpu.make_async_copy(coarse_hbm, coarse_v, osem),
    ]
    small[0].start()
    for j in range(nc):
        load_k(j).start()
    small[1].start()
    small[2].start()
    for j in range(nc):
        load_u(j).start()
    small[0].wait()
    for j in range(nc):
        load_k(j).wait()
    first_v[0] = k_v[0]
    for j in range(nc):
        for q in range(c_v.shape[0]):
            r_v[j, q] = dot(k_v[j], c_v[q]).astype(BF)
    for load in small[1:]:
        load.wait()
    for j in range(nc):
        load_u(j).wait()


def ready(spacing, c, kb, u, trial, coarse):
    nc, _, p, _ = kb.shape
    m = c.shape[0]
    vmem = pl.BlockSpec(memory_space=pltpu.VMEM)
    return pl.pallas_call(
        functools.partial(ready_kernel, spacing),
        out_shape=[
            jax.ShapeDtypeStruct(c.shape, BF),
            jax.ShapeDtypeStruct((nc, p, p), BF),
            jax.ShapeDtypeStruct(u.shape, BF),
            jax.ShapeDtypeStruct(trial.shape, BF),
            jax.ShapeDtypeStruct(coarse.shape, jnp.int32),
            jax.ShapeDtypeStruct((1, p, p), BF),
            jax.ShapeDtypeStruct((nc, m, p, p), BF),
        ],
        in_specs=[pl.BlockSpec(memory_space=pl.ANY)] * 5,
        out_specs=[vmem] * 7,
        scratch_shapes=[pltpu.SemaphoreType.DMA] * 3 + [pltpu.SemaphoreType.DMA((nc,))] * 2,
        compiler_params=pltpu.CompilerParams(vmem_limit_bytes=32 * MIB),
        cost_estimate=pl.CostEstimate(
            flops=20 * nc * m * p**3, bytes_accessed=2 * kb.size, transcendentals=0
        ),
        name="ready",
    )(c, kb, u, trial, coarse)


def rows_kernel(spacing, per, coarse_ref, c_ref, f_ref, r_ref, u_ref, _, out, r_v, o_v, coarse, csem, osem):
    nc, m = r_ref.shape[:2]
    base_j = lax.axis_index("col") * nc
    base_k = lax.axis_index("col") * nc * spacing
    load = pltpu.make_async_copy(coarse_ref, coarse, csem)
    load.start()

    def write(k):
        return pltpu.make_async_copy(o_v.at[k], out.at[k], osem.at[k])

    def rows(i, tail):
        for t in range(per * spacing):
            k = i * spacing + t
            at = coarse[base_k + k] - base_j
            ut = u_ref[k].T
            for q in range(m):
                if tail:
                    block = r_v[jnp.clip(at - (nc - per), 0, per), q]
                else:
                    block = r_ref[jnp.clip(at, 0, nc - 1), q]
                o_v[k, q] = dot(ut, block).astype(BF)
            write(k).start()

    for q in range(m):
        r_v[per, q] = dot(f_ref[0], c_ref[q]).astype(BF)
    for j in range(per):
        r_v[j] = r_ref[nc - per + j]
    load.wait()

    def step(n, carry):
        rows(n * per, False)
        return carry

    lax.fori_loop(0, nc // per - 1, step, 0)
    rows(nc - per, True)
    for k in range(nc * spacing):
        write(k).wait()


def fine_rows(spacing, coarse, c, following, right, u, after):
    rows, p, _ = u.shape
    nc, m = right.shape[:2]
    per = 1
    vmem = pl.BlockSpec(memory_space=pltpu.VMEM)
    return pl.pallas_call(
        functools.partial(rows_kernel, spacing, per),
        out_shape=jax.ShapeDtypeStruct((rows, m, p, p), BF),
        in_specs=[vmem] * 5 + [pl.BlockSpec(memory_space=pl.ANY)],
        out_specs=pl.BlockSpec(memory_space=pl.ANY),
        scratch_shapes=[
            pltpu.VMEM((per + 1, m, p, p), BF),
            pltpu.VMEM((rows, m, p, p), BF),
            pltpu.SMEM(coarse.shape, jnp.int32),
            pltpu.SemaphoreType.DMA,
            pltpu.SemaphoreType.DMA((rows,)),
        ],
        compiler_params=pltpu.CompilerParams(vmem_limit_bytes=38 * MIB),
        cost_estimate=pl.CostEstimate(
            flops=2 * rows * m * p**3, bytes_accessed=2 * rows * m * p * p, transcendentals=0
        ),
        name="fine_rows",
    )(coarse, c, following, right, u, after)


def shares_kernel(lows, n_row, n_col, c_ref, k_ref, f_ref, t_ref, own_ref, *refs):
    sends, w_v = refs[: n_row - 1], refs[-1]
    m, nv = t_ref.shape[:2]
    nc = k_ref.shape[0]
    s = two_terms(sum(dot(t_ref[q], c_ref[q], NT) for q in range(m)))
    each, half = nv // n_col, n_col // 2
    at = lax.broadcasted_iota(jnp.int32, (nv, nv), 1)
    block = lax.div(at, each)
    source = lax.bitwise_xor(lax.axis_index("col"), 2 * lax.rem(block, half) + lax.div(block, half))
    place = source * each + lax.rem(at, each)
    order = (place == lax.broadcasted_iota(jnp.int32, (nv, nv), 0)).astype(F32).astype(BF)
    s = jnp.concatenate([dot(order, s[:nv]), dot(order, s[nv:])], axis=0).astype(BF)
    for j in range(nc + 1):
        w_v[j] = folded_dot(s, k_ref[j] if j < nc else f_ref[0], NT)
    me = lax.axis_index("row")
    (own, spacing), width = lows
    own_ref[...] = w_v[pl.ds(me * own // spacing, width)]
    for n in range(1, n_row):
        other = lax.bitwise_xor(me, n)
        sends[n - 1][...] = w_v[pl.ds(other * own // spacing, width)].astype(BF)


def shares(lows, n_row, n_col, c, kb, following, t):
    nv, p = t.shape[1:]
    width = lows[1]
    vmem = pl.BlockSpec(memory_space=pltpu.VMEM)
    return pl.pallas_call(
        functools.partial(shares_kernel, lows, n_row, n_col),
        out_shape=[jax.ShapeDtypeStruct((width, nv, p), F32)]
        + [jax.ShapeDtypeStruct((width, nv, p), BF)] * (n_row - 1),
        in_specs=[vmem] * 4,
        out_specs=[vmem] * n_row,
        scratch_shapes=[pltpu.VMEM((kb.shape[0] + 1, nv, p), F32)],
        compiler_params=pltpu.CompilerParams(vmem_limit_bytes=16 * MIB),
        name="row_shares",
    )(c, kb, following, t)


def applied_kernel(lows, n_row, nc, spacing, coarse_ref, u_ref, own_ref, *refs):
    got = refs[: n_row - 1]
    out, w_v, coarse, csem = refs[-4:]
    (own, _), width = lows
    load = pltpu.make_async_copy(coarse_ref, coarse, csem)
    load.start()
    me = lax.axis_index("row")
    base_j = lax.axis_index("col") * nc + me * own // spacing
    base_k = lax.axis_index("col") * nc * spacing + me * own
    w = own_ref[...]
    for ref in got:
        w = w + ref[...].astype(F32)
    for i in range(width):
        w_v[i] = two_terms(w[i])
    load.wait()
    for t in range(own):
        at = jnp.clip(coarse[base_k + t] - base_j, 0, width - 1)
        out[t] = folded_dot(w_v[at], u_ref[me * own + t]).astype(BF)


def applied_rows(lows, n_row, nc, spacing, coarse, u, own_share, got):
    width, nv, p = own_share.shape
    vmem = pl.BlockSpec(memory_space=pltpu.VMEM)
    return pl.pallas_call(
        functools.partial(applied_kernel, lows, n_row, nc, spacing),
        out_shape=jax.ShapeDtypeStruct((lows[0][0], nv, p), BF),
        in_specs=[vmem] * (n_row + 2),
        out_specs=vmem,
        scratch_shapes=[
            pltpu.VMEM((width, 2 * nv, p), BF),
            pltpu.SMEM(coarse.shape, jnp.int32),
            pltpu.SemaphoreType.DMA,
        ],
        compiler_params=pltpu.CompilerParams(vmem_limit_bytes=24 * MIB),
        name="applied_rows",
    )(coarse, u, own_share, *got)


def swap(x, by):
    n = lax.axis_size("col")
    return lax.ppermute(x, "col", [(i, i ^ by) for i in range(n)])


def per_device(kb, u, c, trial, coarse):
    n_row, n_col = lax.axis_size("row"), lax.axis_size("col")
    nc, rows = kb.shape[0], u.shape[0]
    spacing = rows // nc
    own = rows // n_row
    width = max((r * own + own - 1) // spacing + 2 - r * own // spacing for r in range(n_row))
    lows = ((own, spacing), width)
    others = [swap(trial, by) for by in range(2, n_col, 2)]
    c, blocks, u, trial, coarse, first, right = ready(spacing, *[pltpu.with_memory_space_constraint(x, pltpu.HBM) for x in (c, kb, u, trial, coarse)])
    half = jnp.concatenate([trial] + others, axis=1)
    full = jnp.concatenate([half, swap(half, 1)], axis=1)
    following = lax.ppermute(first, "col", [(i + 1, i) for i in range(n_col - 1)])
    own_share, *sends = shares(lows, n_row, n_col, c, blocks, following, full)
    got = [lax.ppermute(x, "row", [(i, i ^ (n + 1)) for i in range(n_row)]) for n, x in enumerate(sends)]
    fine = fine_rows(spacing, coarse, c, following, right, u, own_share)
    applied = applied_rows(lows, n_row, nc, spacing, coarse, u, own_share, got)
    return fine, applied


def solution(mesh):
    in_specs = (
        P("col", "row", None, None),
        P("col", None, None),
        P("row", None, None),
        P("row", "col", None),
        P(),
    )
    out_specs = (P("col", "row", None, None), P(("col", "row"), None, None))
    return jax.shard_map(
        per_device, mesh=mesh, in_specs=in_specs, out_specs=out_specs, check_vma=False
    )
```

time: 41.2 us -> 34.8 us (0.84)
  the two profiles are of different devices: /device:TPU:0 before, /device:TPU:1 now
where the time goes in v2:
time: 34.8 us; the launch traced here: 34.6 us
  Pallas kernels  20.4 us (59%)
  starting transfers between devices  10.4 us (30%)
  waiting for transfers between devices  2.98 us (9%)
  between operations  0.76 us (2%)
    pallas_call x1, Pallas kernels, fine_rows(): pl.pallas_call(functools.partial(rows_kernel, spacing, per), out_shape=ja...  12.4 us
    pallas_call x1, Pallas kernels, ready(): pl.pallas_call(functools.partial(ready_kernel, spacing), out_shape=[jax.S...  4.98 us
    ppermute x4, starting transfers between devices, swap(): return lax.ppermute(x, 'col', [(i, i ^ by) for i in range(n)])  4.57 us
    ppermute x1, starting transfers between devices, per_device(): lax.ppermute(first, 'col', [(i + 1, i) for i in range(n_col - 1)])  3.14 us
    ppermute x3, starting transfers between devices, per_device(): lax.ppermute(x, 'row', [(i, i ^ n + 1) for i in range(n_row)])  2.71 us
    pallas_call x1, Pallas kernels, applied_rows(): pl.pallas_call(functools.partial(applied_kernel, lows, n_row, nc, spacing...  1.87 us
    ppermute x1, waiting for transfers between devices, per_device(): lax.ppermute(first, 'col', [(i + 1, i) for i in range(n_col - 1)])  1.76 us
    ppermute x4, waiting for transfers between devices, swap(): return lax.ppermute(x, 'col', [(i, i ^ by) for i in range(n)])  1.21 us
  transfers between devices with their start and end apart: 8, of which 2 were waited for; matrix products, arithmetic and copies ran while one was open for 0% of the time, Pallas kernels for 50%

profile of v2, /device:TPU:1, one launch (start us, length us, event | category | flops | bytes accessed | tf_op | source)
XLA Modules:
  0.0 34.6 jit_solution(7295896262076010649)
XLA Ops:
  0.6 2.2 %collective-permute-start.1 = (bf16[4,8,256]{2,1,0:T(8,128)(2,1)}, bf16[4,8,256]{2,1,0:T(8,128)(2,1)S(1)}, u32[]{:S(2)}, u32[]{:S(2)}) collective-permute-start(bf16[4,8,256]{2,1,0:T(8,128)(2,1)} %t_hbm.1), channel_id=1, source_target_pairs={{0,2},{1,3},{2,0},{3,1},{4,6},{5,7},{6,4},{7,5},{8,10},{9,11},{10,... | collective-permute-start | bytes 49160 | tf_op jit(solution)/shard_map/ppermute | solution.py:236
  2.8 2.3 %collective-permute-start.2 = (bf16[4,8,256]{2,1,0:T(8,128)(2,1)}, bf16[4,8,256]{2,1,0:T(8,128)(2,1)S(1)}, u32[]{:S(2)}, u32[]{:S(2)}) collective-permute-start(bf16[4,8,256]{2,1,0:T(8,128)(2,1)} %t_hbm.1), channel_id=1, source_target_pairs={{0,4},{1,5},{2,6},{3,7},{4,0},{5,1},{6,2},{7,3},{8,12},{9,13},{10,... | collective-permute-start | bytes 49160 | tf_op jit(solution)/shard_map/ppermute | solution.py:236
  5.1 0.0 collective-permute-start.3
  5.1 5.0 %ready.1 = (bf16[4,256,256]{2,1,0:T(8,128)(2,1)S(1)}, bf16[8,256,256]{2,1,0:T(8,128)(2,1)S(1)}, bf16[64,256,256]{2,1,0:T(8,128)(2,1)S(1)}, bf16[4,8,256]{2,1,0:T...) custom-call(bf16[4,256,256]{2,1,0:T(8,128)(2,1)} %c_hbm.1, ...), custom_call_target="tpu_custom_call" | custom-call | flops 10737418240 | bytes 1048576 | tf_op jit(solution)/shard_map/ready/pallas_call | solution.py:72
  10.1 3.1 %collective-permute-start = (bf16[1,256,256]{2,1,0:T(8,128)(2,1)S(1)}, bf16[1,256,256]{2,1,0:T(8,128)(2,1)S(1)}, u32[]{:S(2)}, u32[]{:S(2)}) collective-permute-start(bf16[1,256,256]{2,1,0:T(8,128)(2,1)S(1)} %get-tuple-element.15), channel_id=1, source_target_pairs={{1,0},{2,1},{3,2},{4,3},{5,4},{6,5},{7,6},{9,8},{10,9},{11,10},{12... | collective-permute-start | bytes 393224 | tf_op jit(solution)/shard_map/ppermute | solution.py:250
  13.3 0.0 collective-permute-done.1
  13.3 0.0 collective-permute-done.2
  13.3 0.0 collective-permute-done.3
  13.3 0.1 collective-permute-start.4
  13.4 1.2 %collective-permute-done.4 = bf16[4,32,256]{2,1,0:T(8,128)(2,1)S(1)} collective-permute-done((bf16[4,32,256]{2,1,0:T(8,128)(2,1)S(1)}, bf16[4,32,256]{2,1,0:T(8,128)(2,1)S(1)}, u32[]{:S(2)}, u32[]{:S(2)}) %collective-permute-start.4) | collective-permute-done | bytes 65568 | tf_op jit(solution)/shard_map/ppermute | solution.py:236
  14.7 1.8 %collective-permute-done.f_ref = bf16[1,256,256]{2,1,0:T(8,128)(2,1)S(1)} collective-permute-done((bf16[1,256,256]{2,1,0:T(8,128)(2,1)S(1)}, bf16[1,256,256]{2,1,0:T(8,128)(2,1)S(1)}, u32[]{:S(2)}, u32[]{:S(2)}) %collective-permute-start) | collective-permute-done | bytes 131104 | tf_op jit(solution)/shard_map/ppermute | solution.py:250
  16.4 1.1 %row_shares.1 = (f32[3,64,256]{2,1,0:T(8,128)S(1)}, bf16[3,64,256]{2,1,0:T(8,128)(2,1)S(1)}, bf16[3,64,256]{2,1,0:T(8,128)(2,1)S(1)}, bf16[3,64,256]{2,1,0:T(8,128)(2,1)S(1)}) custom-call(bf16[4,256,256]{2,1,0:T(8,128)(2,1)S(1)} %get-tuple-element.14.c_ref, bf16[8,256,256]{2,1,0:T(8,128)(2,1)S(1)} %get-tuple-element.18.k_ref, ...), custom_call_target="tpu_custom_call" | custom-call | tf_op jit(solution)/shard_map/row_shares/pallas_call | solution.py:184
  17.5 1.3 %collective-permute-start.5 = (bf16[3,64,256]{2,1,0:T(8,128)(2,1)S(1)}, bf16[3,64,256]{2,1,0:T(8,128)(2,1)S(1)}, u32[]{:S(2)}, u32[]{:S(2)}) collective-permute-start(bf16[3,64,256]{2,1,0:T(8,128)(2,1)S(1)} %get-tuple-element.21), channel_id=1, source_target_pairs={{0,8},{8,0},{16,24},{24,16},{1,9},{9,1},{17,25},{25,17},{2,10},{10... | collective-permute-start | bytes 294920 | tf_op jit(solution)/shard_map/ppermute | solution.py:252
  18.8 1.2 %collective-permute-start.6 = (bf16[3,64,256]{2,1,0:T(8,128)(2,1)S(1)}, bf16[3,64,256]{2,1,0:T(8,128)(2,1)S(1)}, u32[]{:S(2)}, u32[]{:S(2)}) collective-permute-start(bf16[3,64,256]{2,1,0:T(8,128)(2,1)S(1)} %get-tuple-element.22), channel_id=1, source_target_pairs={{0,16},{8,24},{16,0},{24,8},{1,17},{9,25},{17,1},{25,9},{2,18},{10... | collective-permute-start | bytes 294920 | tf_op jit(solution)/shard_map/ppermute | solution.py:252
  20.1 0.2 collective-permute-start.7
  20.3 12.4 %fine_rows.1 = bf16[64,4,256,256]{3,2,1,0:T(8,128)(2,1)} custom-call(s32[512]{0:T(512)S(1)} %get-tuple-element.13.coarse_ref, bf16[4,256,256]{2,1,0:T(8,128)(2,1)S(1)} %get-tuple-element.14.c_ref, bf16[1,256,256]{2,1,0:T(8,128)(2,1)S(1)} %collective-permute-done.f_ref, bf16[8,4,256,256]{3,2,1,0:T(8,128)(2,1)S(1)} %get-tuple-element.16.r_ref, ...), custom_call_target="tpu_custom_call" | custom-call | flops 8589934592 | bytes 33554432 | tf_op jit(solution)/shard_map/fine_rows/pallas_call | solution.py:138
  32.6 0.0 collective-permute-done.5.refs_0_
  32.7 0.0 collective-permute-done.6.refs_1_
  32.7 0.0 collective-permute-done.7.refs_2_
  32.7 1.9 %applied_rows.1 = bf16[16,64,256]{2,1,0:T(8,128)(2,1)} custom-call(s32[512]{0:T(512)S(1)} %get-tuple-element.13.coarse_ref, bf16[64,256,256]{2,1,0:T(8,128)(2,1)S(1)} %get-tuple-element.17.u_ref, f32[3,64,256]{2,1,0:T(8,128)S(1)} %get-tuple-element.20._.own_ref, bf16[3,64,256]{2,1,0:T(8,128)(2,1)S(1)} %collective-permute-done.5.refs_0_, ...), custom_call_target="tpu_custom_call" | custom-call | tf_op jit(solution)/shard_map/applied_rows/pallas_call | solution.py:219
  (6 shorter events, 0.0 us)
Async XLA Ops:
  0.6 12.7 %collective-permute-start.1 = (bf16[4,8,256]{2,1,0:T(8,128)(2,1)}, bf16[4,8,256]{2,1,0:T(8,128)(2,1)S(1)}, u32[]{:S(2)}, u32[]{:S(2)}) collective-permute-start(bf16[4,8,256]{2,1,0:T(8,128)(2,1)} %t_hbm.1), channel_id=1, source_target_pairs={{0,2},{1,3},{2,0},{3,1},{4,6},{5,7},{6,4},{7,5},{8,10},{9,11},{10,... | collective-permute-start | bytes 49160 | tf_op jit(solution)/shard_map/ppermute | solution.py:236
  2.8 10.5 %collective-permute-start.2 = (bf16[4,8,256]{2,1,0:T(8,128)(2,1)}, bf16[4,8,256]{2,1,0:T(8,128)(2,1)S(1)}, u32[]{:S(2)}, u32[]{:S(2)}) collective-permute-start(bf16[4,8,256]{2,1,0:T(8,128)(2,1)} %t_hbm.1), channel_id=1, source_target_pairs={{0,4},{1,5},{2,6},{3,7},{4,0},{5,1},{6,2},{7,3},{8,12},{9,13},{10,... | collective-permute-start | bytes 49160 | tf_op jit(solution)/shard_map/ppermute | solution.py:236
  5.1 8.2 %collective-permute-start.3 = (bf16[4,8,256]{2,1,0:T(8,128)(2,1)}, bf16[4,8,256]{2,1,0:T(8,128)(2,1)S(1)}, u32[]{:S(2)}, u32[]{:S(2)}) collective-permute-start(bf16[4,8,256]{2,1,0:T(8,128)(2,1)} %t_hbm.1), channel_id=1, source_target_pairs={{0,6},{1,7},{2,4},{3,5},{4,2},{5,3},{6,0},{7,1},{8,14},{9,15},{10,... | collective-permute-start | bytes 49160 | tf_op jit(solution)/shard_map/ppermute | solution.py:236
  10.1 6.3 %collective-permute-start = (bf16[1,256,256]{2,1,0:T(8,128)(2,1)S(1)}, bf16[1,256,256]{2,1,0:T(8,128)(2,1)S(1)}, u32[]{:S(2)}, u32[]{:S(2)}) collective-permute-start(bf16[1,256,256]{2,1,0:T(8,128)(2,1)S(1)} %get-tuple-element.15), channel_id=1, source_target_pairs={{1,0},{2,1},{3,2},{4,3},{5,4},{6,5},{7,6},{9,8},{10,9},{11,10},{12... | collective-permute-start | bytes 393224 | tf_op jit(solution)/shard_map/ppermute | solution.py:250
  13.3 1.3 %collective-permute-start.4 = (bf16[4,32,256]{2,1,0:T(8,128)(2,1)S(1)}, bf16[4,32,256]{2,1,0:T(8,128)(2,1)S(1)}, u32[]{:S(2)}, u32[]{:S(2)}) collective-permute-start(bf16[4,32,256]{2,1,0:T(8,128)(2,1)S(1)} %pad_maximum_fusion), channel_id=1, source_target_pairs={{0,1},{1,0},{2,3},{3,2},{4,5},{5,4},{6,7},{7,6},{8,9},{9,8},{10,11... | collective-permute-start | bytes 196616 | tf_op jit(solution)/shard_map/ppermute | solution.py:236
  17.5 15.1 %collective-permute-start.5 = (bf16[3,64,256]{2,1,0:T(8,128)(2,1)S(1)}, bf16[3,64,256]{2,1,0:T(8,128)(2,1)S(1)}, u32[]{:S(2)}, u32[]{:S(2)}) collective-permute-start(bf16[3,64,256]{2,1,0:T(8,128)(2,1)S(1)} %get-tuple-element.21), channel_id=1, source_target_pairs={{0,8},{8,0},{16,24},{24,16},{1,9},{9,1},{17,25},{25,17},{2,10},{10... | collective-permute-start | bytes 294920 | tf_op jit(solution)/shard_map/ppermute | solution.py:252
  18.8 13.8 %collective-permute-start.6 = (bf16[3,64,256]{2,1,0:T(8,128)(2,1)S(1)}, bf16[3,64,256]{2,1,0:T(8,128)(2,1)S(1)}, u32[]{:S(2)}, u32[]{:S(2)}) collective-permute-start(bf16[3,64,256]{2,1,0:T(8,128)(2,1)S(1)} %get-tuple-element.22), channel_id=1, source_target_pairs={{0,16},{8,24},{16,0},{24,8},{1,17},{9,25},{17,1},{25,9},{2,18},{10... | collective-permute-start | bytes 294920 | tf_op jit(solution)/shard_map/ppermute | solution.py:252
  20.1 12.6 %collective-permute-start.7 = (bf16[3,64,256]{2,1,0:T(8,128)(2,1)S(1)}, bf16[3,64,256]{2,1,0:T(8,128)(2,1)S(1)}, u32[]{:S(2)}, u32[]{:S(2)}) collective-permute-start(bf16[3,64,256]{2,1,0:T(8,128)(2,1)S(1)} %get-tuple-element.23), channel_id=1, source_target_pairs={{0,24},{8,16},{16,8},{24,0},{1,25},{9,17},{17,9},{25,1},{2,26},{10... | collective-permute-start | bytes 294920 | tf_op jit(solution)/shard_map/ppermute | solution.py:252

commit v3 on v2

--- a/solution.py
+++ b/solution.py
@@ -30,65 +30,56 @@
     return z[:half] + z[half:]
 
 
-def ready_kernel(spacing, c_hbm, k_hbm, u_hbm, t_hbm, coarse_hbm, c_v, k_v, u_v, t_v, coarse_v, first_v, r_v, csem, tsem, osem, ksem, usem):
-    nc = k_hbm.shape[0]
-
-    def load_k(j):
-        return pltpu.make_async_copy(k_hbm.at[j, 0], k_v.at[j], ksem.at[j])
-
-    def load_u(j):
-        here = pl.ds(j * spacing, spacing)
-        return pltpu.make_async_copy(u_hbm.at[here], u_v.at[here], usem.at[j])
-
-    small = [
-        pltpu.make_async_copy(c_hbm, c_v, csem),
+def ready_kernel(k_hbm, t_hbm, coarse_hbm, first_v, t_v, coarse_v, ksem, tsem, csem):
+    loads = [
+        pltpu.make_async_copy(k_hbm.at[0], first_v, ksem),
         pltpu.make_async_copy(t_hbm, t_v, tsem),
-        pltpu.make_async_copy(coarse_hbm, coarse_v, osem),
+        pltpu.make_async_copy(coarse_hbm, coarse_v, csem),
     ]
-    small[0].start()
-    for j in range(nc):
-        load_k(j).start()
-    small[1].start()
-    small[2].start()
-    for j in range(nc):
-        load_u(j).start()
-    small[0].wait()
-    for j in range(nc):
-        load_k(j).wait()
-    first_v[0] = k_v[0]
-    for j in range(nc):
-        for q in range(c_v.shape[0]):
-            r_v[j, q] = dot(k_v[j], c_v[q]).astype(BF)
-    for load in small[1:]:
+    for load in loads:
+        load.start()
+    for load in loads:
         load.wait()
-    for j in range(nc):
-        load_u(j).wait()
-
-
-def ready(spacing, c, kb, u, trial, coarse):
+
+
+def ready(kb, trial, coarse, work):
+    vmem = pl.BlockSpec(memory_space=pltpu.VMEM)
+    held = [pltpu.with_memory_space_constraint(x, pltpu.HBM) for x in (kb, trial, coarse)]
+    return pl.pallas_call(
+        ready_kernel,
+        out_shape=[
+            jax.ShapeDtypeStruct(kb.shape[1:], BF),
+            jax.ShapeDtypeStruct(trial.shape, BF),
+            jax.ShapeDtypeStruct(coarse.shape, jnp.int32),
+        ],
+        in_specs=[pl.BlockSpec(memory_space=pl.ANY)] * 3,
+        out_specs=[vmem] * 3,
+        scratch_shapes=[pltpu.SemaphoreType.DMA] * 3,
+        compiler_params=pltpu.CompilerParams(vmem_limit_bytes=32 * MIB),
+        cost_estimate=pl.CostEstimate(flops=work, bytes_accessed=2 * kb.size, transcendentals=0),
+        name="ready",
+    )(*held)
+
+
+def right_kernel(c_ref, k_ref, _, r_ref):
+    for j in range(k_ref.shape[0]):
+        for q in range(c_ref.shape[0]):
+            r_ref[j, q] = dot(k_ref[j, 0], c_ref[q]).astype(BF)
+
+
+def right_blocks(c, kb, after):
     nc, _, p, _ = kb.shape
     m = c.shape[0]
     vmem = pl.BlockSpec(memory_space=pltpu.VMEM)
     return pl.pallas_call(
-        functools.partial(ready_kernel, spacing),
-        out_shape=[
-            jax.ShapeDtypeStruct(c.shape, BF),
-            jax.ShapeDtypeStruct((nc, p, p), BF),
-            jax.ShapeDtypeStruct(u.shape, BF),
-            jax.ShapeDtypeStruct(trial.shape, BF),
-            jax.ShapeDtypeStruct(coarse.shape, jnp.int32),
-            jax.ShapeDtypeStruct((1, p, p), BF),
-            jax.ShapeDtypeStruct((nc, m, p, p), BF),
-        ],
-        in_specs=[pl.BlockSpec(memory_space=pl.ANY)] * 5,
-        out_specs=[vmem] * 7,
-        scratch_shapes=[pltpu.SemaphoreType.DMA] * 3 + [pltpu.SemaphoreType.DMA((nc,))] * 2,
+        right_kernel,
+        out_shape=jax.ShapeDtypeStruct((nc, m, p, p), BF),
+        in_specs=[vmem] * 2 + [pl.BlockSpec(memory_space=pl.ANY)],
+        out_specs=vmem,
         compiler_params=pltpu.CompilerParams(vmem_limit_bytes=32 * MIB),
-        cost_estimate=pl.CostEstimate(
-            flops=20 * nc * m * p**3, bytes_accessed=2 * kb.size, transcendentals=0
-        ),
-        name="ready",
-    )(c, kb, u, trial, coarse)
+        cost_estimate=pl.CostEstimate(flops=2 * nc * m * p**3, bytes_accessed=0, transcendentals=0),
+        name="right_blocks",
+    )(c, kb, after)
 
 
 def rows_kernel(spacing, per, coarse_ref, c_ref, f_ref, r_ref, u_ref, _, out, r_v, o_v, coarse, csem, osem):
@@ -133,7 +124,7 @@
 def fine_rows(spacing, coarse, c, following, right, u, after):
     rows, p, _ = u.shape
     nc, m = right.shape[:2]
-    per = 1
+    per = 2 if nc % 2 == 0 else 1
     vmem = pl.BlockSpec(memory_space=pltpu.VMEM)
     return pl.pallas_call(
         functools.partial(rows_kernel, spacing, per),
@@ -163,12 +154,14 @@
     each, half = nv // n_col, n_col // 2
     at = lax.broadcasted_iota(jnp.int32, (nv, nv), 1)
     block = lax.div(at, each)
-    source = lax.bitwise_xor(lax.axis_index("col"), 2 * lax.rem(block, half) + lax.div(block, half))
+    source = lax.bitwise_xor(
+        lax.axis_index("col"), lax.rem(n_col - 2 * lax.rem(block, half), n_col) + lax.div(block, half)
+    )
     place = source * each + lax.rem(at, each)
     order = (place == lax.broadcasted_iota(jnp.int32, (nv, nv), 0)).astype(F32).astype(BF)
     s = jnp.concatenate([dot(order, s[:nv]), dot(order, s[nv:])], axis=0).astype(BF)
     for j in range(nc + 1):
-        w_v[j] = folded_dot(s, k_ref[j] if j < nc else f_ref[0], NT)
+        w_v[j] = folded_dot(s, k_ref[j, 0] if j < nc else f_ref[0], NT)
     me = lax.axis_index("row")
     (own, spacing), width = lows
     own_ref[...] = w_v[pl.ds(me * own // spacing, width)]
@@ -195,7 +188,7 @@
 
 def applied_kernel(lows, n_row, nc, spacing, coarse_ref, u_ref, own_ref, *refs):
     got = refs[: n_row - 1]
-    out, w_v, coarse, csem = refs[-4:]
+    out, w_v, o_v, coarse, csem, osem = refs[-6:]
     (own, _), width = lows
     load = pltpu.make_async_copy(coarse_ref, coarse, csem)
     load.start()
@@ -208,9 +201,19 @@
     for i in range(width):
         w_v[i] = two_terms(w[i])
     load.wait()
+    part = min(4, own)
+
+    def write(t):
+        here = pl.ds(t, part)
+        return pltpu.make_async_copy(o_v.at[here], out.at[here], osem.at[t])
+
     for t in range(own):
         at = jnp.clip(coarse[base_k + t] - base_j, 0, width - 1)
-        out[t] = folded_dot(w_v[at], u_ref[me * own + t]).astype(BF)
+        o_v[t] = folded_dot(w_v[at], u_ref[me * own + t]).astype(BF)
+        if (t + 1) % part == 0:
+            write(t + 1 - part).start()
+    for t in range(0, own, part):
+        write(t).wait()
 
 
 def applied_rows(lows, n_row, nc, spacing, coarse, u, own_share, got):
@@ -220,11 +223,13 @@
         functools.partial(applied_kernel, lows, n_row, nc, spacing),
         out_shape=jax.ShapeDtypeStruct((lows[0][0], nv, p), BF),
         in_specs=[vmem] * (n_row + 2),
-        out_specs=vmem,
+        out_specs=pl.BlockSpec(memory_space=pl.ANY),
         scratch_shapes=[
             pltpu.VMEM((width, 2 * nv, p), BF),
+            pltpu.VMEM((lows[0][0], nv, p), BF),
             pltpu.SMEM(coarse.shape, jnp.int32),
             pltpu.SemaphoreType.DMA,
+            pltpu.SemaphoreType.DMA((lows[0][0],)),
         ],
         compiler_params=pltpu.CompilerParams(vmem_limit_bytes=24 * MIB),
         name="applied_rows",
@@ -243,12 +248,14 @@
     own = rows // n_row
     width = max((r * own + own - 1) // spacing + 2 - r * own // spacing for r in range(n_row))
     lows = ((own, spacing), width)
-    others = [swap(trial, by) for by in range(2, n_col, 2)]
-    c, blocks, u, trial, coarse, first, right = ready(spacing, *[pltpu.with_memory_space_constraint(x, pltpu.HBM) for x in (c, kb, u, trial, coarse)])
+    others = [swap(trial, by) for by in range(n_col - 2, 0, -2)]
+    work = 12 * nc * c.shape[0] * c.shape[1] ** 3
+    first, trial, coarse = ready(kb, trial, coarse, work)
     half = jnp.concatenate([trial] + others, axis=1)
+    right = right_blocks(c, kb, half)
     full = jnp.concatenate([half, swap(half, 1)], axis=1)
     following = lax.ppermute(first, "col", [(i + 1, i) for i in range(n_col - 1)])
-    own_share, *sends = shares(lows, n_row, n_col, c, blocks, following, full)
+    own_share, *sends = shares(lows, n_row, n_col, c, kb, following, full)
     got = [lax.ppermute(x, "row", [(i, i ^ (n + 1)) for i in range(n_row)]) for n, x in enumerate(sends)]
     fine = fine_rows(spacing, coarse, c, following, right, u, own_share)
     applied = applied_rows(lows, n_row, nc, spacing, coarse, u, own_share, got)

time: 34.8 us -> 31.7 us (0.911)
  Pallas kernels: 20.4 us -> 17.7 us
  waiting for transfers between devices: 2.98 us -> 1.34 us
  starting transfers between devices: 10.4 us -> 11.6 us
    pallas_call x1 -> x2, Pallas kernels: 4.98 us -> 2.34 us  [the longest x1 1.26 us: right_blocks(): pl.pallas_call(right_kernel, out_shape=jax.ShapeDtypeStruct((nc, m, p, p)...]
    ppermute x4, waiting for transfers between devices: 1.21 us -> 0.01 us  [swap(): return lax.ppermute(x, 'col', [(i, i ^ by) for i in range(n)])]
    ppermute x4, starting transfers between devices: 4.57 us -> 5.51 us  [swap(): return lax.ppermute(x, 'col', [(i, i ^ by) for i in range(n)])]
    ppermute x1, waiting for transfers between devices: 1.76 us -> 1.32 us  [per_device(): lax.ppermute(first, 'col', [(i + 1, i) for i in range(n_col - 1)])]
  transfers between devices with their start and end apart: 8 -> 8, of which waited for: 2 -> 1; matrix products, arithmetic and copies ran while one was open for 0% -> 0% of each run, Pallas kernels for 50% -> 47%
where the time goes in v3:
time: 31.7 us; the launch traced here: 31.5 us
  Pallas kernels  17.7 us (56%)
  starting transfers between devices  11.6 us (37%)
  waiting for transfers between devices  1.34 us (4%)
  between operations  0.79 us (2%)
    pallas_call x1, Pallas kernels, fine_rows(): pl.pallas_call(functools.partial(rows_kernel, spacing, per), out_shape=ja...  12.4 us
    ppermute x4, starting transfers between devices, swap(): return lax.ppermute(x, 'col', [(i, i ^ by) for i in range(n)])  5.51 us
    ppermute x1, starting transfers between devices, per_device(): lax.ppermute(first, 'col', [(i + 1, i) for i in range(n_col - 1)])  3.41 us
    ppermute x3, starting transfers between devices, per_device(): lax.ppermute(x, 'row', [(i, i ^ n + 1) for i in range(n_row)])  2.71 us
    pallas_call x1, Pallas kernels, applied_rows(): pl.pallas_call(functools.partial(applied_kernel, lows, n_row, nc, spacing...  1.88 us
    ppermute x1, waiting for transfers between devices, per_device(): lax.ppermute(first, 'col', [(i + 1, i) for i in range(n_col - 1)])  1.32 us
    pallas_call x1, Pallas kernels, right_blocks(): pl.pallas_call(right_kernel, out_shape=jax.ShapeDtypeStruct((nc, m, p, p)...  1.26 us
    pallas_call x1, Pallas kernels, shares(): pl.pallas_call(functools.partial(shares_kernel, lows, n_row, n_col), out_...  1.13 us
  transfers between devices with their start and end apart: 8, of which 1 were waited for; matrix products, arithmetic and copies ran while one was open for 0% of the time, Pallas kernels for 47%

profile of v3, /device:TPU:1, one launch (start us, length us, event | category | flops | bytes accessed | tf_op | source)
XLA Modules:
  0.0 31.5 jit_solution(6383168512043020557)
XLA Ops:
  0.6 0.0 copy-start.2
  0.6 0.0 copy-start.1
  0.7 4.2 %collective-permute-start.1 = (bf16[4,8,256]{2,1,0:T(8,128)(2,1)}, bf16[4,8,256]{2,1,0:T(8,128)(2,1)S(1)}, u32[]{:S(2)}, u32[]{:S(2)}) collective-permute-start(bf16[4,8,256]{2,1,0:T(8,128)(2,1)} %t_hbm.1), channel_id=1, source_target_pairs={{0,6},{1,7},{2,4},{3,5},{4,2},{5,3},{6,0},{7,1},{8,14},{9,15},{10,... | collective-permute-start | bytes 49160 | tf_op jit(solution)/shard_map/ppermute | solution.py:241
  4.9 0.0 collective-permute-start.2
  4.9 0.4 %collective-permute-start.3 = (bf16[4,8,256]{2,1,0:T(8,128)(2,1)}, bf16[4,8,256]{2,1,0:T(8,128)(2,1)S(1)}, u32[]{:S(2)}, u32[]{:S(2)}) collective-permute-start(bf16[4,8,256]{2,1,0:T(8,128)(2,1)} %t_hbm.1), channel_id=1, source_target_pairs={{0,2},{1,3},{2,0},{3,1},{4,6},{5,7},{6,4},{7,5},{8,10},{9,11},{10,... | collective-permute-start | bytes 49160 | tf_op jit(solution)/shard_map/ppermute | solution.py:241
  5.2 0.0 copy-start
  5.2 1.1 %ready.1 = (bf16[1,256,256]{2,1,0:T(8,128)(2,1)S(1)}, bf16[4,8,256]{2,1,0:T(8,128)(2,1)S(1)}, s32[512]{0:T(512)S(1)}) custom-call(bf16[8,1,256,256]{3,2,1,0:T(8,128)(2,1)} %k_ref.3, bf16[4,8,256]{2,1,0:T(8,128)(2,1)} %t_hbm.1, s32[512]{0:T(512)} %coarse_hbm.1), custom_call_target="tpu_custom_call" | custom-call | flops 6442450944 | bytes 1048576 | tf_op jit(solution)/shard_map/ready/pallas_call | solution.py:48
  6.3 3.4 %collective-permute-start = (bf16[1,256,256]{2,1,0:T(8,128)(2,1)S(1)}, bf16[1,256,256]{2,1,0:T(8,128)(2,1)S(1)}, u32[]{:S(2)}, u32[]{:S(2)}) collective-permute-start(bf16[1,256,256]{2,1,0:T(8,128)(2,1)S(1)} %get-tuple-element.10), channel_id=1, source_target_pairs={{1,0},{2,1},{3,2},{4,3},{5,4},{6,5},{7,6},{9,8},{10,9},{11,10},{12... | collective-permute-start | bytes 393224 | tf_op jit(solution)/shard_map/ppermute | solution.py:257
  9.8 0.0 collective-permute-done.1
  9.8 0.0 collective-permute-done.2
  9.8 0.0 collective-permute-done.3
  9.8 0.9 %collective-permute-start.4 = (bf16[4,32,256]{2,1,0:T(8,128)(2,1)S(1)}, bf16[4,32,256]{2,1,0:T(8,128)(2,1)S(1)}, u32[]{:S(2)}, u32[]{:S(2)}) collective-permute-start(bf16[4,32,256]{2,1,0:T(8,128)(2,1)S(1)} %get-tuple-element.17._), channel_id=1, source_target_pairs={{0,1},{1,0},{2,3},{3,2},{4,5},{5,4},{6,7},{7,6},{8,9},{9,8},{10,11... | collective-permute-start | bytes 196616 | tf_op jit(solution)/shard_map/ppermute | solution.py:241
  10.8 0.0 copy-done.2
  10.8 0.0 copy-done.1
  10.8 1.3 %right_blocks.1.r_ref = bf16[8,4,256,256]{3,2,1,0:T(8,128)(2,1)S(1)} custom-call(bf16[4,256,256]{2,1,0:T(8,128)(2,1)S(1)} %copy-done.1, bf16[8,1,256,256]{3,2,1,0:T(8,128)(2,1)S(1)} %copy-done.2, bf16[4,32,256]{2,1,0:T(8,128)(2,1)S(1)} %get-tuple-element.17._), custom_call_target="tpu_custom_call" | custom-call | flops 1073741824 | tf_op jit(solution)/shard_map/right_blocks/pallas_call | solution.py:74
  12.0 0.0 collective-permute-done.4
  12.0 1.3 %collective-permute-done.f_ref = bf16[1,256,256]{2,1,0:T(8,128)(2,1)S(1)} collective-permute-done((bf16[1,256,256]{2,1,0:T(8,128)(2,1)S(1)}, bf16[1,256,256]{2,1,0:T(8,128)(2,1)S(1)}, u32[]{:S(2)}, u32[]{:S(2)}) %collective-permute-start) | collective-permute-done | bytes 131104 | tf_op jit(solution)/shard_map/ppermute | solution.py:257
  13.4 1.1 %row_shares.1 = (f32[3,64,256]{2,1,0:T(8,128)S(1)}, bf16[3,64,256]{2,1,0:T(8,128)(2,1)S(1)}, bf16[3,64,256]{2,1,0:T(8,128)(2,1)S(1)}, bf16[3,64,256]{2,1,0:T(8,128)(2,1)S(1)}) custom-call(bf16[4,256,256]{2,1,0:T(8,128)(2,1)S(1)} %copy-done.1, bf16[8,1,256,256]{3,2,1,0:T(8,128)(2,1)S(1)} %copy-done.2, bf16[1,256,256]{2,1,0:T(8,128)(2,1)S(1)} %collective-permute-done.f_ref, ...), custom_call_target="tpu_custom_call" | custom-call | tf_op jit(solution)/shard_map/row_shares/pallas_call | solution.py:177
  14.5 1.3 %collective-permute-start.5 = (bf16[3,64,256]{2,1,0:T(8,128)(2,1)S(1)}, bf16[3,64,256]{2,1,0:T(8,128)(2,1)S(1)}, u32[]{:S(2)}, u32[]{:S(2)}) collective-permute-start(bf16[3,64,256]{2,1,0:T(8,128)(2,1)S(1)} %get-tuple-element.13), channel_id=1, source_target_pairs={{0,8},{8,0},{16,24},{24,16},{1,9},{9,1},{17,25},{25,17},{2,10},{10... | collective-permute-start | bytes 294920 | tf_op jit(solution)/shard_map/ppermute | solution.py:259
  15.8 1.2 %collective-permute-start.6 = (bf16[3,64,256]{2,1,0:T(8,128)(2,1)S(1)}, bf16[3,64,256]{2,1,0:T(8,128)(2,1)S(1)}, u32[]{:S(2)}, u32[]{:S(2)}) collective-permute-start(bf16[3,64,256]{2,1,0:T(8,128)(2,1)S(1)} %get-tuple-element.14), channel_id=1, source_target_pairs={{0,16},{8,24},{16,0},{24,8},{1,17},{9,25},{17,1},{25,9},{2,18},{10... | collective-permute-start | bytes 294920 | tf_op jit(solution)/shard_map/ppermute | solution.py:259
  17.0 0.2 collective-permute-start.7
  17.2 0.0 copy-done
  17.2 12.4 %fine_rows.1 = bf16[64,4,256,256]{3,2,1,0:T(8,128)(2,1)} custom-call(s32[512]{0:T(512)S(1)} %get-tuple-element.9.coarse_ref, bf16[4,256,256]{2,1,0:T(8,128)(2,1)S(1)} %copy-done.1, bf16[1,256,256]{2,1,0:T(8,128)(2,1)S(1)} %collective-permute-done.f_ref, bf16[8,4,256,256]{3,2,1,0:T(8,128)(2,1)S(1)} %right_blocks.1.r_ref, bf16[64,256,256]{2,1,0:T(8,128)(2,1)S(1)} %copy-done, ...), custom_call_target="tpu_custom_call" | custom-call | flops 8589934592 | bytes 33554432 | tf_op jit(solution)/shard_map/fine_rows/pallas_call | solution.py:129
  29.6 0.0 collective-permute-done.5.refs_0_
  29.6 0.0 collective-permute-done.6.refs_1_
  29.6 0.0 collective-permute-done.7.refs_2_
  29.6 1.9 %applied_rows.1 = bf16[16,64,256]{2,1,0:T(8,128)(2,1)} custom-call(s32[512]{0:T(512)S(1)} %get-tuple-element.9.coarse_ref, bf16[64,256,256]{2,1,0:T(8,128)(2,1)S(1)} %copy-done, f32[3,64,256]{2,1,0:T(8,128)S(1)} %get-tuple-element.12._.own_ref, bf16[3,64,256]{2,1,0:T(8,128)(2,1)S(1)} %collective-permute-done.5.refs_0_, ...), custom_call_target="tpu_custom_call" | custom-call | tf_op jit(solution)/shard_map/applied_rows/pallas_call | solution.py:222
  (5 shorter events, 0.0 us)
Async XLA Ops:
  0.6 10.1 %copy-start.2 = (bf16[8,1,256,256]{3,2,1,0:T(8,128)(2,1)S(1)}, bf16[8,1,256,256]{3,2,1,0:T(8,128)(2,1)}, u32[]{:S(2)}) copy-start(bf16[8,1,256,256]{3,2,1,0:T(8,128)(2,1)} %k_ref.3) | copy-start | bytes 3145732
  0.6 10.1 %copy-start.1 = (bf16[4,256,256]{2,1,0:T(8,128)(2,1)S(1)}, bf16[4,256,256]{2,1,0:T(8,128)(2,1)}, u32[]{:S(2)}) copy-start(bf16[4,256,256]{2,1,0:T(8,128)(2,1)} %c_ref.5) | copy-start | bytes 1572868
  0.7 9.1 %collective-permute-start.1 = (bf16[4,8,256]{2,1,0:T(8,128)(2,1)}, bf16[4,8,256]{2,1,0:T(8,128)(2,1)S(1)}, u32[]{:S(2)}, u32[]{:S(2)}) collective-permute-start(bf16[4,8,256]{2,1,0:T(8,128)(2,1)} %t_hbm.1), channel_id=1, source_target_pairs={{0,6},{1,7},{2,4},{3,5},{4,2},{5,3},{6,0},{7,1},{8,14},{9,15},{10,... | collective-permute-start | bytes 49160 | tf_op jit(solution)/shard_map/ppermute | solution.py:241
  4.9 4.9 %collective-permute-start.2 = (bf16[4,8,256]{2,1,0:T(8,128)(2,1)}, bf16[4,8,256]{2,1,0:T(8,128)(2,1)S(1)}, u32[]{:S(2)}, u32[]{:S(2)}) collective-permute-start(bf16[4,8,256]{2,1,0:T(8,128)(2,1)} %t_hbm.1), channel_id=1, source_target_pairs={{0,4},{1,5},{2,6},{3,7},{4,0},{5,1},{6,2},{7,3},{8,12},{9,13},{10,... | collective-permute-start | bytes 49160 | tf_op jit(solution)/shard_map/ppermute | solution.py:241
  4.9 4.9 %collective-permute-start.3 = (bf16[4,8,256]{2,1,0:T(8,128)(2,1)}, bf16[4,8,256]{2,1,0:T(8,128)(2,1)S(1)}, u32[]{:S(2)}, u32[]{:S(2)}) collective-permute-start(bf16[4,8,256]{2,1,0:T(8,128)(2,1)} %t_hbm.1), channel_id=1, source_target_pairs={{0,2},{1,3},{2,0},{3,1},{4,6},{5,7},{6,4},{7,5},{8,10},{9,11},{10,... | collective-permute-start | bytes 49160 | tf_op jit(solution)/shard_map/ppermute | solution.py:241
  5.2 12.0 %copy-start = (bf16[64,256,256]{2,1,0:T(8,128)(2,1)S(1)}, bf16[64,256,256]{2,1,0:T(8,128)(2,1)}, u32[]{:S(2)}) copy-start(bf16[64,256,256]{2,1,0:T(8,128)(2,1)} %u_ref.3) | copy-start | bytes 25165828
  6.3 7.0 %collective-permute-start = (bf16[1,256,256]{2,1,0:T(8,128)(2,1)S(1)}, bf16[1,256,256]{2,1,0:T(8,128)(2,1)S(1)}, u32[]{:S(2)}, u32[]{:S(2)}) collective-permute-start(bf16[1,256,256]{2,1,0:T(8,128)(2,1)S(1)} %get-tuple-element.10), channel_id=1, source_target_pairs={{1,0},{2,1},{3,2},{4,3},{5,4},{6,5},{7,6},{9,8},{10,9},{11,10},{12... | collective-permute-start | bytes 393224 | tf_op jit(solution)/shard_map/ppermute | solution.py:257
  9.8 2.2 %collective-permute-start.4 = (bf16[4,32,256]{2,1,0:T(8,128)(2,1)S(1)}, bf16[4,32,256]{2,1,0:T(8,128)(2,1)S(1)}, u32[]{:S(2)}, u32[]{:S(2)}) collective-permute-start(bf16[4,32,256]{2,1,0:T(8,128)(2,1)S(1)} %get-tuple-element.17._), channel_id=1, source_target_pairs={{0,1},{1,0},{2,3},{3,2},{4,5},{5,4},{6,7},{7,6},{8,9},{9,8},{10,11... | collective-permute-start | bytes 196616 | tf_op jit(solution)/shard_map/ppermute | solution.py:241
  14.5 15.1 %collective-permute-start.5 = (bf16[3,64,256]{2,1,0:T(8,128)(2,1)S(1)}, bf16[3,64,256]{2,1,0:T(8,128)(2,1)S(1)}, u32[]{:S(2)}, u32[]{:S(2)}) collective-permute-start(bf16[3,64,256]{2,1,0:T(8,128)(2,1)S(1)} %get-tuple-element.13), channel_id=1, source_target_pairs={{0,8},{8,0},{16,24},{24,16},{1,9},{9,1},{17,25},{25,17},{2,10},{10... | collective-permute-start | bytes 294920 | tf_op jit(solution)/shard_map/ppermute | solution.py:259
  15.8 13.8 %collective-permute-start.6 = (bf16[3,64,256]{2,1,0:T(8,128)(2,1)S(1)}, bf16[3,64,256]{2,1,0:T(8,128)(2,1)S(1)}, u32[]{:S(2)}, u32[]{:S(2)}) collective-permute-start(bf16[3,64,256]{2,1,0:T(8,128)(2,1)S(1)} %get-tuple-element.14), channel_id=1, source_target_pairs={{0,16},{8,24},{16,0},{24,8},{1,17},{9,25},{17,1},{25,9},{2,18},{10... | collective-permute-start | bytes 294920 | tf_op jit(solution)/shard_map/ppermute | solution.py:259
  17.0 12.6 %collective-permute-start.7 = (bf16[3,64,256]{2,1,0:T(8,128)(2,1)S(1)}, bf16[3,64,256]{2,1,0:T(8,128)(2,1)S(1)}, u32[]{:S(2)}, u32[]{:S(2)}) collective-permute-start(bf16[3,64,256]{2,1,0:T(8,128)(2,1)S(1)} %get-tuple-element.15), channel_id=1, source_target_pairs={{0,24},{8,16},{16,8},{24,0},{1,25},{9,17},{17,9},{25,1},{2,26},{10... | collective-permute-start | bytes 294920 | tf_op jit(solution)/shard_map/ppermute | solution.py:259

commit v4 on v3

--- a/solution.py
+++ b/solution.py
@@ -73,7 +73,7 @@
     vmem = pl.BlockSpec(memory_space=pltpu.VMEM)
     return pl.pallas_call(
         right_kernel,
-        out_shape=jax.ShapeDtypeStruct((nc, m, p, p), BF),
+        out_shape=jax.ShapeDtypeStruct((nc + 1, m, p, p), BF),
         in_specs=[vmem] * 2 + [pl.BlockSpec(memory_space=pl.ANY)],
         out_specs=vmem,
         compiler_params=pltpu.CompilerParams(vmem_limit_bytes=32 * MIB),
@@ -82,68 +82,62 @@
     )(c, kb, after)
 
 
-def rows_kernel(spacing, per, coarse_ref, c_ref, f_ref, r_ref, u_ref, _, out, r_v, o_v, coarse, csem, osem):
-    nc, m = r_ref.shape[:2]
+def rows_kernel(spacing, coarse_ref, c_ref, f_ref, _, u_ref, __, out, r_ref, o_v, coarse, csem, osem):
+    nc, m = r_ref.shape[0] - 1, r_ref.shape[1]
     base_j = lax.axis_index("col") * nc
     base_k = lax.axis_index("col") * nc * spacing
+    per = min(2, nc) * spacing
     load = pltpu.make_async_copy(coarse_ref, coarse, csem)
     load.start()
 
     def write(k):
         return pltpu.make_async_copy(o_v.at[k], out.at[k], osem.at[k])
 
-    def rows(i, tail):
-        for t in range(per * spacing):
-            k = i * spacing + t
-            at = coarse[base_k + k] - base_j
+    load.wait()
+
+    def step(i, carry):
+        for t in range(per):
+            k = i * per + t
+            at = jnp.clip(coarse[base_k + k] - base_j, 0, nc)
             ut = u_ref[k].T
             for q in range(m):
-                if tail:
-                    block = r_v[jnp.clip(at - (nc - per), 0, per), q]
-                else:
-                    block = r_ref[jnp.clip(at, 0, nc - 1), q]
-                o_v[k, q] = dot(ut, block).astype(BF)
+                o_v[k, q] = dot(ut, r_ref[at, q]).astype(BF)
             write(k).start()
 
-    for q in range(m):
-        r_v[per, q] = dot(f_ref[0], c_ref[q]).astype(BF)
-    for j in range(per):
-        r_v[j] = r_ref[nc - per + j]
-    load.wait()
-
-    def step(n, carry):
-        rows(n * per, False)
+        @pl.when(i == 0)
+        def _():
+            for q in range(m):
+                r_ref[nc, q] = dot(f_ref[0], c_ref[q]).astype(BF)
+
         return carry
 
-    lax.fori_loop(0, nc // per - 1, step, 0)
-    rows(nc - per, True)
+    lax.fori_loop(0, nc * spacing // per, step, 0)
     for k in range(nc * spacing):
         write(k).wait()
 
 
 def fine_rows(spacing, coarse, c, following, right, u, after):
     rows, p, _ = u.shape
-    nc, m = right.shape[:2]
-    per = 2 if nc % 2 == 0 else 1
-    vmem = pl.BlockSpec(memory_space=pltpu.VMEM)
-    return pl.pallas_call(
-        functools.partial(rows_kernel, spacing, per),
-        out_shape=jax.ShapeDtypeStruct((rows, m, p, p), BF),
+    m = right.shape[1]
+    vmem = pl.BlockSpec(memory_space=pltpu.VMEM)
+    return pl.pallas_call(
+        functools.partial(rows_kernel, spacing),
+        out_shape=[jax.ShapeDtypeStruct((rows, m, p, p), BF), jax.ShapeDtypeStruct(right.shape, BF)],
         in_specs=[vmem] * 5 + [pl.BlockSpec(memory_space=pl.ANY)],
-        out_specs=pl.BlockSpec(memory_space=pl.ANY),
+        out_specs=[pl.BlockSpec(memory_space=pl.ANY), vmem],
         scratch_shapes=[
-            pltpu.VMEM((per + 1, m, p, p), BF),
             pltpu.VMEM((rows, m, p, p), BF),
             pltpu.SMEM(coarse.shape, jnp.int32),
             pltpu.SemaphoreType.DMA,
             pltpu.SemaphoreType.DMA((rows,)),
         ],
+        input_output_aliases={3: 1},
         compiler_params=pltpu.CompilerParams(vmem_limit_bytes=38 * MIB),
         cost_estimate=pl.CostEstimate(
             flops=2 * rows * m * p**3, bytes_accessed=2 * rows * m * p * p, transcendentals=0
         ),
         name="fine_rows",
-    )(coarse, c, following, right, u, after)
+    )(coarse, c, following, right, u, after)[0]
 
 
 def shares_kernel(lows, n_row, n_col, c_ref, k_ref, f_ref, t_ref, own_ref, *refs):

time: 31.7 us -> 31.6 us (level)
  transfers between devices with their start and end apart: 8 -> 8, of which waited for: 1 -> 1; matrix products, arithmetic and copies ran while one was open for 0% -> 0% of each run, Pallas kernels for 47% -> 46%
where the time goes in v4:
time: 31.6 us; the launch traced here: 31.4 us
  Pallas kernels  17.5 us (55%)
  starting transfers between devices  11.8 us (37%)
  waiting for transfers between devices  1.33 us (4%)
  between operations  0.79 us (2%)
    pallas_call x1, Pallas kernels, fine_rows(): pl.pallas_call(functools.partial(rows_kernel, spacing), out_shape=[jax.Sh...  12.3 us
    ppermute x4, starting transfers between devices, swap(): return lax.ppermute(x, 'col', [(i, i ^ by) for i in range(n)])  5.65 us
    ppermute x1, starting transfers between devices, per_device(): lax.ppermute(first, 'col', [(i + 1, i) for i in range(n_col - 1)])  3.41 us
    ppermute x3, starting transfers between devices, per_device(): lax.ppermute(x, 'row', [(i, i ^ n + 1) for i in range(n_row)])  2.71 us
    pallas_call x1, Pallas kernels, applied_rows(): pl.pallas_call(functools.partial(applied_kernel, lows, n_row, nc, spacing...  1.88 us
    ppermute x1, waiting for transfers between devices, per_device(): lax.ppermute(first, 'col', [(i + 1, i) for i in range(n_col - 1)])  1.31 us
    pallas_call x1, Pallas kernels, right_blocks(): pl.pallas_call(right_kernel, out_shape=jax.ShapeDtypeStruct((nc + 1, m, p...  1.26 us
    pallas_call x1, Pallas kernels, shares(): pl.pallas_call(functools.partial(shares_kernel, lows, n_row, n_col), out_...  1.13 us
  transfers between devices with their start and end apart: 8, of which 1 were waited for; matrix products, arithmetic and copies ran while one was open for 0% of the time, Pallas kernels for 46%

profile of v4, /device:TPU:1, one launch (start us, length us, event | category | flops | bytes accessed | tf_op | source)
XLA Modules:
  0.0 31.4 jit_solution(4186774518156375591)
XLA Ops:
  0.6 0.0 copy-start.1
  0.6 0.0 copy-start.2
  0.7 4.2 %collective-permute-start.1 = (bf16[4,8,256]{2,1,0:T(8,128)(2,1)}, bf16[4,8,256]{2,1,0:T(8,128)(2,1)S(1)}, u32[]{:S(2)}, u32[]{:S(2)}) collective-permute-start(bf16[4,8,256]{2,1,0:T(8,128)(2,1)} %t_hbm.1), channel_id=1, source_target_pairs={{0,6},{1,7},{2,4},{3,5},{4,2},{5,3},{6,0},{7,1},{8,14},{9,15},{10,... | collective-permute-start | bytes 49160 | tf_op jit(solution)/shard_map/ppermute | solution.py:235
  4.9 0.0 collective-permute-start.2
  4.9 0.4 %collective-permute-start.3 = (bf16[4,8,256]{2,1,0:T(8,128)(2,1)}, bf16[4,8,256]{2,1,0:T(8,128)(2,1)S(1)}, u32[]{:S(2)}, u32[]{:S(2)}) collective-permute-start(bf16[4,8,256]{2,1,0:T(8,128)(2,1)} %t_hbm.1), channel_id=1, source_target_pairs={{0,2},{1,3},{2,0},{3,1},{4,6},{5,7},{6,4},{7,5},{8,10},{9,11},{10,... | collective-permute-start | bytes 49160 | tf_op jit(solution)/shard_map/ppermute | solution.py:235
  5.2 0.9 %ready.1 = (bf16[1,256,256]{2,1,0:T(8,128)(2,1)S(1)}, bf16[4,8,256]{2,1,0:T(8,128)(2,1)S(1)}, s32[512]{0:T(512)S(1)}) custom-call(bf16[8,1,256,256]{3,2,1,0:T(8,128)(2,1)} %k_ref.3, bf16[4,8,256]{2,1,0:T(8,128)(2,1)} %t_hbm.1, s32[512]{0:T(512)} %coarse_hbm.1), custom_call_target="tpu_custom_call" | custom-call | flops 6442450944 | bytes 1048576 | tf_op jit(solution)/shard_map/ready/pallas_call | solution.py:48
  6.2 0.0 copy-start
  6.2 3.4 %collective-permute-start = (bf16[1,256,256]{2,1,0:T(8,128)(2,1)S(1)}, bf16[1,256,256]{2,1,0:T(8,128)(2,1)S(1)}, u32[]{:S(2)}, u32[]{:S(2)}) collective-permute-start(bf16[1,256,256]{2,1,0:T(8,128)(2,1)S(1)} %get-tuple-element.11), channel_id=1, source_target_pairs={{1,0},{2,1},{3,2},{4,3},{5,4},{6,5},{7,6},{9,8},{10,9},{11,10},{12... | collective-permute-start | bytes 393224 | tf_op jit(solution)/shard_map/ppermute | solution.py:251
  9.6 0.0 collective-permute-done.1
  9.6 0.0 collective-permute-done.2
  9.7 0.0 collective-permute-done.3
  9.7 1.1 %collective-permute-start.4 = (bf16[4,32,256]{2,1,0:T(8,128)(2,1)S(1)}, bf16[4,32,256]{2,1,0:T(8,128)(2,1)S(1)}, u32[]{:S(2)}, u32[]{:S(2)}) collective-permute-start(bf16[4,32,256]{2,1,0:T(8,128)(2,1)S(1)} %get-tuple-element.19._), channel_id=1, source_target_pairs={{0,1},{1,0},{2,3},{3,2},{4,5},{5,4},{6,7},{7,6},{8,9},{9,8},{10,11... | collective-permute-start | bytes 196616 | tf_op jit(solution)/shard_map/ppermute | solution.py:235
  10.8 0.0 copy-done.1
  10.8 0.0 copy-done.2
  10.8 1.3 %right_blocks.1._ = bf16[9,4,256,256]{3,2,1,0:T(8,128)(2,1)S(1)} custom-call(bf16[4,256,256]{2,1,0:T(8,128)(2,1)S(1)} %copy-done.2, bf16[8,1,256,256]{3,2,1,0:T(8,128)(2,1)S(1)} %copy-done.1, bf16[4,32,256]{2,1,0:T(8,128)(2,1)S(1)} %get-tuple-element.19._), custom_call_target="tpu_custom_call" | custom-call | flops 1073741824 | tf_op jit(solution)/shard_map/right_blocks/pallas_call | solution.py:74
  12.0 0.0 collective-permute-done.4
  12.1 1.3 %collective-permute-done.f_ref = bf16[1,256,256]{2,1,0:T(8,128)(2,1)S(1)} collective-permute-done((bf16[1,256,256]{2,1,0:T(8,128)(2,1)S(1)}, bf16[1,256,256]{2,1,0:T(8,128)(2,1)S(1)}, u32[]{:S(2)}, u32[]{:S(2)}) %collective-permute-start) | collective-permute-done | bytes 131104 | tf_op jit(solution)/shard_map/ppermute | solution.py:251
  13.4 1.1 %row_shares.1 = (f32[3,64,256]{2,1,0:T(8,128)S(1)}, bf16[3,64,256]{2,1,0:T(8,128)(2,1)S(1)}, bf16[3,64,256]{2,1,0:T(8,128)(2,1)S(1)}, bf16[3,64,256]{2,1,0:T(8,128)(2,1)S(1)}) custom-call(bf16[4,256,256]{2,1,0:T(8,128)(2,1)S(1)} %copy-done.2, bf16[8,1,256,256]{3,2,1,0:T(8,128)(2,1)S(1)} %copy-done.1, bf16[1,256,256]{2,1,0:T(8,128)(2,1)S(1)} %collective-permute-done.f_ref, ...), custom_call_target="tpu_custom_call" | custom-call | tf_op jit(solution)/shard_map/row_shares/pallas_call | solution.py:171
  14.5 1.3 %collective-permute-start.5 = (bf16[3,64,256]{2,1,0:T(8,128)(2,1)S(1)}, bf16[3,64,256]{2,1,0:T(8,128)(2,1)S(1)}, u32[]{:S(2)}, u32[]{:S(2)}) collective-permute-start(bf16[3,64,256]{2,1,0:T(8,128)(2,1)S(1)} %get-tuple-element.15), channel_id=1, source_target_pairs={{0,8},{8,0},{16,24},{24,16},{1,9},{9,1},{17,25},{25,17},{2,10},{10... | collective-permute-start | bytes 294920 | tf_op jit(solution)/shard_map/ppermute | solution.py:253
  15.8 1.2 %collective-permute-start.6 = (bf16[3,64,256]{2,1,0:T(8,128)(2,1)S(1)}, bf16[3,64,256]{2,1,0:T(8,128)(2,1)S(1)}, u32[]{:S(2)}, u32[]{:S(2)}) collective-permute-start(bf16[3,64,256]{2,1,0:T(8,128)(2,1)S(1)} %get-tuple-element.16), channel_id=1, source_target_pairs={{0,16},{8,24},{16,0},{24,8},{1,17},{9,25},{17,1},{25,9},{2,18},{10... | collective-permute-start | bytes 294920 | tf_op jit(solution)/shard_map/ppermute | solution.py:253
  17.0 0.2 collective-permute-start.7
  17.2 0.0 copy-done
  17.2 12.3 %fine_rows.1 = (bf16[64,4,256,256]{3,2,1,0:T(8,128)(2,1)}, bf16[9,4,256,256]{3,2,1,0:T(8,128)(2,1)S(1)}) custom-call(s32[512]{0:T(512)S(1)} %get-tuple-element.10.coarse_ref, bf16[4,256,256]{2,1,0:T(8,128)(2,1)S(1)} %copy-done.2, bf16[1,256,256]{2,1,0:T(8,128)(2,1)S(1)} %collective-permute-done.f_ref, ...), custom_call_target="tpu_custom_call", output_to_operand_aliasing={{1}: (3, {})} | custom-call | flops 8589934592 | bytes 33554432 | tf_op jit(solution)/shard_map/fine_rows/pallas_call | solution.py:123
  29.5 0.0 collective-permute-done.5.refs_0_
  29.5 0.0 collective-permute-done.6.refs_1_
  29.6 0.0 collective-permute-done.7.refs_2_
  29.6 1.9 %applied_rows.1 = bf16[16,64,256]{2,1,0:T(8,128)(2,1)} custom-call(s32[512]{0:T(512)S(1)} %get-tuple-element.10.coarse_ref, bf16[64,256,256]{2,1,0:T(8,128)(2,1)S(1)} %copy-done, f32[3,64,256]{2,1,0:T(8,128)S(1)} %get-tuple-element.13.__.own_ref, bf16[3,64,256]{2,1,0:T(8,128)(2,1)S(1)} %collective-permute-done.5.refs_0_, ...), custom_call_target="tpu_custom_call" | custom-call | tf_op jit(solution)/shard_map/applied_rows/pallas_call | solution.py:216
  (5 shorter events, 0.0 us)
Async XLA Ops:
  0.6 10.1 %copy-start.1 = (bf16[8,1,256,256]{3,2,1,0:T(8,128)(2,1)S(1)}, bf16[8,1,256,256]{3,2,1,0:T(8,128)(2,1)}, u32[]{:S(2)}) copy-start(bf16[8,1,256,256]{3,2,1,0:T(8,128)(2,1)} %k_ref.3) | copy-start | bytes 3145732
  0.6 10.1 %copy-start.2 = (bf16[4,256,256]{2,1,0:T(8,128)(2,1)S(1)}, bf16[4,256,256]{2,1,0:T(8,128)(2,1)}, u32[]{:S(2)}) copy-start(bf16[4,256,256]{2,1,0:T(8,128)(2,1)} %c_ref.5) | copy-start | bytes 1572868
  0.7 9.0 %collective-permute-start.1 = (bf16[4,8,256]{2,1,0:T(8,128)(2,1)}, bf16[4,8,256]{2,1,0:T(8,128)(2,1)S(1)}, u32[]{:S(2)}, u32[]{:S(2)}) collective-permute-start(bf16[4,8,256]{2,1,0:T(8,128)(2,1)} %t_hbm.1), channel_id=1, source_target_pairs={{0,6},{1,7},{2,4},{3,5},{4,2},{5,3},{6,0},{7,1},{8,14},{9,15},{10,... | collective-permute-start | bytes 49160 | tf_op jit(solution)/shard_map/ppermute | solution.py:235
  4.9 4.8 %collective-permute-start.2 = (bf16[4,8,256]{2,1,0:T(8,128)(2,1)}, bf16[4,8,256]{2,1,0:T(8,128)(2,1)S(1)}, u32[]{:S(2)}, u32[]{:S(2)}) collective-permute-start(bf16[4,8,256]{2,1,0:T(8,128)(2,1)} %t_hbm.1), channel_id=1, source_target_pairs={{0,4},{1,5},{2,6},{3,7},{4,0},{5,1},{6,2},{7,3},{8,12},{9,13},{10,... | collective-permute-start | bytes 49160 | tf_op jit(solution)/shard_map/ppermute | solution.py:235
  4.9 4.8 %collective-permute-start.3 = (bf16[4,8,256]{2,1,0:T(8,128)(2,1)}, bf16[4,8,256]{2,1,0:T(8,128)(2,1)S(1)}, u32[]{:S(2)}, u32[]{:S(2)}) collective-permute-start(bf16[4,8,256]{2,1,0:T(8,128)(2,1)} %t_hbm.1), channel_id=1, source_target_pairs={{0,2},{1,3},{2,0},{3,1},{4,6},{5,7},{6,4},{7,5},{8,10},{9,11},{10,... | collective-permute-start | bytes 49160 | tf_op jit(solution)/shard_map/ppermute | solution.py:235
  6.2 11.0 %copy-start = (bf16[64,256,256]{2,1,0:T(8,128)(2,1)S(1)}, bf16[64,256,256]{2,1,0:T(8,128)(2,1)}, u32[]{:S(2)}) copy-start(bf16[64,256,256]{2,1,0:T(8,128)(2,1)} %u_ref.3) | copy-start | bytes 25165828
  6.2 7.2 %collective-permute-start = (bf16[1,256,256]{2,1,0:T(8,128)(2,1)S(1)}, bf16[1,256,256]{2,1,0:T(8,128)(2,1)S(1)}, u32[]{:S(2)}, u32[]{:S(2)}) collective-permute-start(bf16[1,256,256]{2,1,0:T(8,128)(2,1)S(1)} %get-tuple-element.11), channel_id=1, source_target_pairs={{1,0},{2,1},{3,2},{4,3},{5,4},{6,5},{7,6},{9,8},{10,9},{11,10},{12... | collective-permute-start | bytes 393224 | tf_op jit(solution)/shard_map/ppermute | solution.py:251
  9.7 2.3 %collective-permute-start.4 = (bf16[4,32,256]{2,1,0:T(8,128)(2,1)S(1)}, bf16[4,32,256]{2,1,0:T(8,128)(2,1)S(1)}, u32[]{:S(2)}, u32[]{:S(2)}) collective-permute-start(bf16[4,32,256]{2,1,0:T(8,128)(2,1)S(1)} %get-tuple-element.19._), channel_id=1, source_target_pairs={{0,1},{1,0},{2,3},{3,2},{4,5},{5,4},{6,7},{7,6},{8,9},{9,8},{10,11... | collective-permute-start | bytes 196616 | tf_op jit(solution)/shard_map/ppermute | solution.py:235
  14.5 15.0 %collective-permute-start.5 = (bf16[3,64,256]{2,1,0:T(8,128)(2,1)S(1)}, bf16[3,64,256]{2,1,0:T(8,128)(2,1)S(1)}, u32[]{:S(2)}, u32[]{:S(2)}) collective-permute-start(bf16[3,64,256]{2,1,0:T(8,128)(2,1)S(1)} %get-tuple-element.15), channel_id=1, source_target_pairs={{0,8},{8,0},{16,24},{24,16},{1,9},{9,1},{17,25},{25,17},{2,10},{10... | collective-permute-start | bytes 294920 | tf_op jit(solution)/shard_map/ppermute | solution.py:253
  15.8 13.8 %collective-permute-start.6 = (bf16[3,64,256]{2,1,0:T(8,128)(2,1)S(1)}, bf16[3,64,256]{2,1,0:T(8,128)(2,1)S(1)}, u32[]{:S(2)}, u32[]{:S(2)}) collective-permute-start(bf16[3,64,256]{2,1,0:T(8,128)(2,1)S(1)} %get-tuple-element.16), channel_id=1, source_target_pairs={{0,16},{8,24},{16,0},{24,8},{1,17},{9,25},{17,1},{25,9},{2,18},{10... | collective-permute-start | bytes 294920 | tf_op jit(solution)/shard_map/ppermute | solution.py:253
  17.0 12.5 %collective-permute-start.7 = (bf16[3,64,256]{2,1,0:T(8,128)(2,1)S(1)}, bf16[3,64,256]{2,1,0:T(8,128)(2,1)S(1)}, u32[]{:S(2)}, u32[]{:S(2)}) collective-permute-start(bf16[3,64,256]{2,1,0:T(8,128)(2,1)S(1)} %get-tuple-element.17), channel_id=1, source_target_pairs={{0,24},{8,16},{16,8},{24,0},{1,25},{9,17},{17,9},{25,1},{2,26},{10... | collective-permute-start | bytes 294920 | tf_op jit(solution)/shard_map/ppermute | solution.py:253

commit v5 on v3

--- a/solution.py
+++ b/solution.py
@@ -150,7 +150,8 @@
     sends, w_v = refs[: n_row - 1], refs[-1]
     m, nv = t_ref.shape[:2]
     nc = k_ref.shape[0]
-    s = two_terms(sum(dot(t_ref[q], c_ref[q], NT) for q in range(m)))
+    t = jnp.concatenate([t_ref[q] for q in range(m)], axis=1)
+    s = two_terms(dot(t, jnp.concatenate([c_ref[q] for q in range(m)], axis=1), NT))
     each, half = nv // n_col, n_col // 2
     at = lax.broadcasted_iota(jnp.int32, (nv, nv), 1)
     block = lax.div(at, each)
@@ -159,7 +160,8 @@
     )
     place = source * each + lax.rem(at, each)
     order = (place == lax.broadcasted_iota(jnp.int32, (nv, nv), 0)).astype(F32).astype(BF)
-    s = jnp.concatenate([dot(order, s[:nv]), dot(order, s[nv:])], axis=0).astype(BF)
+    s = dot(order, jnp.concatenate([s[:nv], s[nv:]], axis=1)).astype(BF)
+    s = jnp.concatenate([s[:, : s.shape[1] // 2], s[:, s.shape[1] // 2 :]], axis=0)
     for j in range(nc + 1):
         w_v[j] = folded_dot(s, k_ref[j, 0] if j < nc else f_ref[0], NT)
     me = lax.axis_index("row")

time: 31.7 us -> 31.7 us (level)
  no operation moved by 1% of the time
where the time goes in v5:
time: 31.7 us; the launch traced here: 31.5 us
  Pallas kernels  17.7 us (56%)
  starting transfers between devices  11.6 us (37%)
  waiting for transfers between devices  1.34 us (4%)
  between operations  0.79 us (2%)
    pallas_call x1, Pallas kernels, fine_rows(): pl.pallas_call(functools.partial(rows_kernel, spacing, per), out_shape=ja...  12.4 us
    ppermute x4, starting transfers between devices, swap(): return lax.ppermute(x, 'col', [(i, i ^ by) for i in range(n)])  5.51 us
    ppermute x1, starting transfers between devices, per_device(): lax.ppermute(first, 'col', [(i + 1, i) for i in range(n_col - 1)])  3.41 us
    ppermute x3, starting transfers between devices, per_device(): lax.ppermute(x, 'row', [(i, i ^ n + 1) for i in range(n_row)])  2.71 us
    pallas_call x1, Pallas kernels, applied_rows(): pl.pallas_call(functools.partial(applied_kernel, lows, n_row, nc, spacing...  1.88 us
    ppermute x1, waiting for transfers between devices, per_device(): lax.ppermute(first, 'col', [(i + 1, i) for i in range(n_col - 1)])  1.32 us
    pallas_call x1, Pallas kernels, right_blocks(): pl.pallas_call(right_kernel, out_shape=jax.ShapeDtypeStruct((nc, m, p, p)...  1.26 us
    pallas_call x1, Pallas kernels, shares(): pl.pallas_call(functools.partial(shares_kernel, lows, n_row, n_col), out_...  1.13 us
  transfers between devices with their start and end apart: 8, of which 1 were waited for; matrix products, arithmetic and copies ran while one was open for 0% of the time, Pallas kernels for 47%

profile of v5, /device:TPU:1, one launch (start us, length us, event | category | flops | bytes accessed | tf_op | source)
XLA Modules:
  0.0 31.5 jit_solution(4945920406556085746)
XLA Ops:
  0.6 0.0 copy-start.2
  0.6 0.0 copy-start.1
  0.7 4.2 %collective-permute-start.1 = (bf16[4,8,256]{2,1,0:T(8,128)(2,1)}, bf16[4,8,256]{2,1,0:T(8,128)(2,1)S(1)}, u32[]{:S(2)}, u32[]{:S(2)}) collective-permute-start(bf16[4,8,256]{2,1,0:T(8,128)(2,1)} %t_hbm.1), channel_id=1, source_target_pairs={{0,6},{1,7},{2,4},{3,5},{4,2},{5,3},{6,0},{7,1},{8,14},{9,15},{10,... | collective-permute-start | bytes 49160 | tf_op jit(solution)/shard_map/ppermute | solution.py:243
  4.9 0.0 collective-permute-start.2
  4.9 0.4 %collective-permute-start.3 = (bf16[4,8,256]{2,1,0:T(8,128)(2,1)}, bf16[4,8,256]{2,1,0:T(8,128)(2,1)S(1)}, u32[]{:S(2)}, u32[]{:S(2)}) collective-permute-start(bf16[4,8,256]{2,1,0:T(8,128)(2,1)} %t_hbm.1), channel_id=1, source_target_pairs={{0,2},{1,3},{2,0},{3,1},{4,6},{5,7},{6,4},{7,5},{8,10},{9,11},{10,... | collective-permute-start | bytes 49160 | tf_op jit(solution)/shard_map/ppermute | solution.py:243
  5.2 0.0 copy-start
  5.2 1.1 %ready.1 = (bf16[1,256,256]{2,1,0:T(8,128)(2,1)S(1)}, bf16[4,8,256]{2,1,0:T(8,128)(2,1)S(1)}, s32[512]{0:T(512)S(1)}) custom-call(bf16[8,1,256,256]{3,2,1,0:T(8,128)(2,1)} %k_ref.3, bf16[4,8,256]{2,1,0:T(8,128)(2,1)} %t_hbm.1, s32[512]{0:T(512)} %coarse_hbm.1), custom_call_target="tpu_custom_call" | custom-call | flops 6442450944 | bytes 1048576 | tf_op jit(solution)/shard_map/ready/pallas_call | solution.py:48
  6.3 3.4 %collective-permute-start = (bf16[1,256,256]{2,1,0:T(8,128)(2,1)S(1)}, bf16[1,256,256]{2,1,0:T(8,128)(2,1)S(1)}, u32[]{:S(2)}, u32[]{:S(2)}) collective-permute-start(bf16[1,256,256]{2,1,0:T(8,128)(2,1)S(1)} %get-tuple-element.10), channel_id=1, source_target_pairs={{1,0},{2,1},{3,2},{4,3},{5,4},{6,5},{7,6},{9,8},{10,9},{11,10},{12... | collective-permute-start | bytes 393224 | tf_op jit(solution)/shard_map/ppermute | solution.py:259
  9.8 0.0 collective-permute-done.1
  9.8 0.0 collective-permute-done.2
  9.8 0.0 collective-permute-done.3
  9.8 0.9 %collective-permute-start.4 = (bf16[4,32,256]{2,1,0:T(8,128)(2,1)S(1)}, bf16[4,32,256]{2,1,0:T(8,128)(2,1)S(1)}, u32[]{:S(2)}, u32[]{:S(2)}) collective-permute-start(bf16[4,32,256]{2,1,0:T(8,128)(2,1)S(1)} %get-tuple-element.17._), channel_id=1, source_target_pairs={{0,1},{1,0},{2,3},{3,2},{4,5},{5,4},{6,7},{7,6},{8,9},{9,8},{10,11... | collective-permute-start | bytes 196616 | tf_op jit(solution)/shard_map/ppermute | solution.py:243
  10.8 0.0 copy-done.2
  10.8 0.0 copy-done.1
  10.8 1.3 %right_blocks.1.r_ref = bf16[8,4,256,256]{3,2,1,0:T(8,128)(2,1)S(1)} custom-call(bf16[4,256,256]{2,1,0:T(8,128)(2,1)S(1)} %copy-done.1, bf16[8,1,256,256]{3,2,1,0:T(8,128)(2,1)S(1)} %copy-done.2, bf16[4,32,256]{2,1,0:T(8,128)(2,1)S(1)} %get-tuple-element.17._), custom_call_target="tpu_custom_call" | custom-call | flops 1073741824 | tf_op jit(solution)/shard_map/right_blocks/pallas_call | solution.py:74
  12.0 0.0 collective-permute-done.4
  12.0 1.3 %collective-permute-done.f_ref = bf16[1,256,256]{2,1,0:T(8,128)(2,1)S(1)} collective-permute-done((bf16[1,256,256]{2,1,0:T(8,128)(2,1)S(1)}, bf16[1,256,256]{2,1,0:T(8,128)(2,1)S(1)}, u32[]{:S(2)}, u32[]{:S(2)}) %collective-permute-start) | collective-permute-done | bytes 131104 | tf_op jit(solution)/shard_map/ppermute | solution.py:259
  13.4 1.1 %row_shares.1 = (f32[3,64,256]{2,1,0:T(8,128)S(1)}, bf16[3,64,256]{2,1,0:T(8,128)(2,1)S(1)}, bf16[3,64,256]{2,1,0:T(8,128)(2,1)S(1)}, bf16[3,64,256]{2,1,0:T(8,128)(2,1)S(1)}) custom-call(bf16[4,256,256]{2,1,0:T(8,128)(2,1)S(1)} %copy-done.1, bf16[8,1,256,256]{3,2,1,0:T(8,128)(2,1)S(1)} %copy-done.2, bf16[1,256,256]{2,1,0:T(8,128)(2,1)S(1)} %collective-permute-done.f_ref, ...), custom_call_target="tpu_custom_call" | custom-call | tf_op jit(solution)/shard_map/row_shares/pallas_call | solution.py:179
  14.5 1.3 %collective-permute-start.5 = (bf16[3,64,256]{2,1,0:T(8,128)(2,1)S(1)}, bf16[3,64,256]{2,1,0:T(8,128)(2,1)S(1)}, u32[]{:S(2)}, u32[]{:S(2)}) collective-permute-start(bf16[3,64,256]{2,1,0:T(8,128)(2,1)S(1)} %get-tuple-element.13), channel_id=1, source_target_pairs={{0,8},{8,0},{16,24},{24,16},{1,9},{9,1},{17,25},{25,17},{2,10},{10... | collective-permute-start | bytes 294920 | tf_op jit(solution)/shard_map/ppermute | solution.py:261
  15.8 1.2 %collective-permute-start.6 = (bf16[3,64,256]{2,1,0:T(8,128)(2,1)S(1)}, bf16[3,64,256]{2,1,0:T(8,128)(2,1)S(1)}, u32[]{:S(2)}, u32[]{:S(2)}) collective-permute-start(bf16[3,64,256]{2,1,0:T(8,128)(2,1)S(1)} %get-tuple-element.14), channel_id=1, source_target_pairs={{0,16},{8,24},{16,0},{24,8},{1,17},{9,25},{17,1},{25,9},{2,18},{10... | collective-permute-start | bytes 294920 | tf_op jit(solution)/shard_map/ppermute | solution.py:261
  17.0 0.2 collective-permute-start.7
  17.2 0.0 copy-done
  17.2 12.4 %fine_rows.1 = bf16[64,4,256,256]{3,2,1,0:T(8,128)(2,1)} custom-call(s32[512]{0:T(512)S(1)} %get-tuple-element.9.coarse_ref, bf16[4,256,256]{2,1,0:T(8,128)(2,1)S(1)} %copy-done.1, bf16[1,256,256]{2,1,0:T(8,128)(2,1)S(1)} %collective-permute-done.f_ref, bf16[8,4,256,256]{3,2,1,0:T(8,128)(2,1)S(1)} %right_blocks.1.r_ref, bf16[64,256,256]{2,1,0:T(8,128)(2,1)S(1)} %copy-done, ...), custom_call_target="tpu_custom_call" | custom-call | flops 8589934592 | bytes 33554432 | tf_op jit(solution)/shard_map/fine_rows/pallas_call | solution.py:129
  29.6 0.0 collective-permute-done.5.refs_0_
  29.6 0.0 collective-permute-done.6.refs_1_
  29.6 0.0 collective-permute-done.7.refs_2_
  29.6 1.9 %applied_rows.1 = bf16[16,64,256]{2,1,0:T(8,128)(2,1)} custom-call(s32[512]{0:T(512)S(1)} %get-tuple-element.9.coarse_ref, bf16[64,256,256]{2,1,0:T(8,128)(2,1)S(1)} %copy-done, f32[3,64,256]{2,1,0:T(8,128)S(1)} %get-tuple-element.12._.own_ref, bf16[3,64,256]{2,1,0:T(8,128)(2,1)S(1)} %collective-permute-done.5.refs_0_, ...), custom_call_target="tpu_custom_call" | custom-call | tf_op jit(solution)/shard_map/applied_rows/pallas_call | solution.py:224
  (5 shorter events, 0.0 us)
Async XLA Ops:
  0.6 10.1 %copy-start.2 = (bf16[8,1,256,256]{3,2,1,0:T(8,128)(2,1)S(1)}, bf16[8,1,256,256]{3,2,1,0:T(8,128)(2,1)}, u32[]{:S(2)}) copy-start(bf16[8,1,256,256]{3,2,1,0:T(8,128)(2,1)} %k_ref.3) | copy-start | bytes 3145732
  0.6 10.1 %copy-start.1 = (bf16[4,256,256]{2,1,0:T(8,128)(2,1)S(1)}, bf16[4,256,256]{2,1,0:T(8,128)(2,1)}, u32[]{:S(2)}) copy-start(bf16[4,256,256]{2,1,0:T(8,128)(2,1)} %c_ref.5) | copy-start | bytes 1572868
  0.7 9.1 %collective-permute-start.1 = (bf16[4,8,256]{2,1,0:T(8,128)(2,1)}, bf16[4,8,256]{2,1,0:T(8,128)(2,1)S(1)}, u32[]{:S(2)}, u32[]{:S(2)}) collective-permute-start(bf16[4,8,256]{2,1,0:T(8,128)(2,1)} %t_hbm.1), channel_id=1, source_target_pairs={{0,6},{1,7},{2,4},{3,5},{4,2},{5,3},{6,0},{7,1},{8,14},{9,15},{10,... | collective-permute-start | bytes 49160 | tf_op jit(solution)/shard_map/ppermute | solution.py:243
  4.9 4.9 %collective-permute-start.2 = (bf16[4,8,256]{2,1,0:T(8,128)(2,1)}, bf16[4,8,256]{2,1,0:T(8,128)(2,1)S(1)}, u32[]{:S(2)}, u32[]{:S(2)}) collective-permute-start(bf16[4,8,256]{2,1,0:T(8,128)(2,1)} %t_hbm.1), channel_id=1, source_target_pairs={{0,4},{1,5},{2,6},{3,7},{4,0},{5,1},{6,2},{7,3},{8,12},{9,13},{10,... | collective-permute-start | bytes 49160 | tf_op jit(solution)/shard_map/ppermute | solution.py:243
  4.9 4.9 %collective-permute-start.3 = (bf16[4,8,256]{2,1,0:T(8,128)(2,1)}, bf16[4,8,256]{2,1,0:T(8,128)(2,1)S(1)}, u32[]{:S(2)}, u32[]{:S(2)}) collective-permute-start(bf16[4,8,256]{2,1,0:T(8,128)(2,1)} %t_hbm.1), channel_id=1, source_target_pairs={{0,2},{1,3},{2,0},{3,1},{4,6},{5,7},{6,4},{7,5},{8,10},{9,11},{10,... | collective-permute-start | bytes 49160 | tf_op jit(solution)/shard_map/ppermute | solution.py:243
  5.2 12.0 %copy-start = (bf16[64,256,256]{2,1,0:T(8,128)(2,1)S(1)}, bf16[64,256,256]{2,1,0:T(8,128)(2,1)}, u32[]{:S(2)}) copy-start(bf16[64,256,256]{2,1,0:T(8,128)(2,1)} %u_ref.3) | copy-start | bytes 25165828
  6.3 7.0 %collective-permute-start = (bf16[1,256,256]{2,1,0:T(8,128)(2,1)S(1)}, bf16[1,256,256]{2,1,0:T(8,128)(2,1)S(1)}, u32[]{:S(2)}, u32[]{:S(2)}) collective-permute-start(bf16[1,256,256]{2,1,0:T(8,128)(2,1)S(1)} %get-tuple-element.10), channel_id=1, source_target_pairs={{1,0},{2,1},{3,2},{4,3},{5,4},{6,5},{7,6},{9,8},{10,9},{11,10},{12... | collective-permute-start | bytes 393224 | tf_op jit(solution)/shard_map/ppermute | solution.py:259
  9.8 2.2 %collective-permute-start.4 = (bf16[4,32,256]{2,1,0:T(8,128)(2,1)S(1)}, bf16[4,32,256]{2,1,0:T(8,128)(2,1)S(1)}, u32[]{:S(2)}, u32[]{:S(2)}) collective-permute-start(bf16[4,32,256]{2,1,0:T(8,128)(2,1)S(1)} %get-tuple-element.17._), channel_id=1, source_target_pairs={{0,1},{1,0},{2,3},{3,2},{4,5},{5,4},{6,7},{7,6},{8,9},{9,8},{10,11... | collective-permute-start | bytes 196616 | tf_op jit(solution)/shard_map/ppermute | solution.py:243
  14.5 15.1 %collective-permute-start.5 = (bf16[3,64,256]{2,1,0:T(8,128)(2,1)S(1)}, bf16[3,64,256]{2,1,0:T(8,128)(2,1)S(1)}, u32[]{:S(2)}, u32[]{:S(2)}) collective-permute-start(bf16[3,64,256]{2,1,0:T(8,128)(2,1)S(1)} %get-tuple-element.13), channel_id=1, source_target_pairs={{0,8},{8,0},{16,24},{24,16},{1,9},{9,1},{17,25},{25,17},{2,10},{10... | collective-permute-start | bytes 294920 | tf_op jit(solution)/shard_map/ppermute | solution.py:261
  15.8 13.8 %collective-permute-start.6 = (bf16[3,64,256]{2,1,0:T(8,128)(2,1)S(1)}, bf16[3,64,256]{2,1,0:T(8,128)(2,1)S(1)}, u32[]{:S(2)}, u32[]{:S(2)}) collective-permute-start(bf16[3,64,256]{2,1,0:T(8,128)(2,1)S(1)} %get-tuple-element.14), channel_id=1, source_target_pairs={{0,16},{8,24},{16,0},{24,8},{1,17},{9,25},{17,1},{25,9},{2,18},{10... | collective-permute-start | bytes 294920 | tf_op jit(solution)/shard_map/ppermute | solution.py:261
  17.0 12.6 %collective-permute-start.7 = (bf16[3,64,256]{2,1,0:T(8,128)(2,1)S(1)}, bf16[3,64,256]{2,1,0:T(8,128)(2,1)S(1)}, u32[]{:S(2)}, u32[]{:S(2)}) collective-permute-start(bf16[3,64,256]{2,1,0:T(8,128)(2,1)S(1)} %get-tuple-element.15), channel_id=1, source_target_pairs={{0,24},{8,16},{16,8},{24,0},{1,25},{9,17},{17,9},{25,1},{2,26},{10... | collective-permute-start | bytes 294920 | tf_op jit(solution)/shard_map/ppermute | solution.py:261
